TPU v7x, 32 devices: a whole 2x2x4 slice. The times are simulated.
32 devices in a mesh: regions: 16 (over z, y, x), shard: 2 (over core).
Axes of the slice: x: 2, y: 2, z: 4, core: 2. Of those that a mesh axis runs over, the one named last changes fastest.
Arguments:
- layer_in: bfloat16 [2, 9216, 768], P('shard', 'regions'), may hold values from -6 to 6
- out_grad: bfloat16 [2, 9216, 768], P('shard', 'regions'), may hold values from -6 to 6
- w_qkv: bfloat16 [768, 2304], P(('regions', 'shard')), may hold values from -0.21875 to 0.21875
- w_out: bfloat16 [768, 768], P(('regions', 'shard')), may hold values from -0.875 to 0.875
- w_up: bfloat16 [768, 3072], P(('regions', 'shard')), may hold values from -0.21875 to 0.21875
- w_down: bfloat16 [3072, 768], P(('regions', 'shard')), may hold values from -0.109375 to 0.109375
- vectors: bfloat16 [12, 768], P(None, ('regions', 'shard')), may hold values from 0.5 to 1.5
- relative: float32 [12, 253], replicated, may hold values from -3 to 3
- first_qkv: float32 [768, 2304], P(('regions', 'shard')), may hold values from -6 to 6
- second_qkv: float32 [768, 2304], P(('regions', 'shard')), may hold values from 0.5 to 50
- first_out: float32 [768, 768], P(('regions', 'shard')), may hold values from -6 to 6
- second_out: float32 [768, 768], P(('regions', 'shard')), may hold values from 0.05 to 5
- first_up: float32 [768, 3072], P(('regions', 'shard')), may hold values from -6 to 6
- second_up: float32 [768, 3072], P(('regions', 'shard')), may hold values from 0.5 to 50
- first_down: float32 [3072, 768], P(('regions', 'shard')), may hold values from -6 to 6
- second_down: float32 [3072, 768], P(('regions', 'shard')), may hold values from 0.5 to 50
- first_vectors: float32 [12, 768], P(None, ('regions', 'shard')), may hold values from -6 to 6
- second_vectors: float32 [12, 768], P(None, ('regions', 'shard')), may hold values from 0.5 to 50
- first_relative: float32 [12, 253], replicated, may hold values from -6 to 6
- second_relative: float32 [12, 253], replicated, may hold values from 0.05 to 5
- token_slot: int32 [2, 9216], P('shard', 'regions'), may hold values from 0 to 1151, as said below
- home_index: int32 [2, 9216], P('shard', 'regions'), may hold values from 0 to 1151, as said below
- box_x: int32 [2, 9216], P('shard', 'regions'), may hold values from 0 to 31
- box_y: int32 [2, 9216], P('shard', 'regions'), may hold values from 0 to 31
Outputs:
- layer_out: bfloat16 [2, 9216, 768], P('shard', 'regions')
- in_grad: float32 [2, 9216, 768], P('shard', 'regions')
- grad_qkv: float32 [768, 2304], P(('regions', 'shard'))
- firsts_qkv: float32 [768, 2304], P(('regions', 'shard'))
- seconds_qkv: float32 [768, 2304], P(('regions', 'shard'))
- update_qkv: float32 [768, 2304], P(('regions', 'shard'))
- grad_out: float32 [768, 768], P(('regions', 'shard'))
- firsts_out: float32 [768, 768], P(('regions', 'shard'))
- seconds_out: float32 [768, 768], P(('regions', 'shard'))
- update_out: float32 [768, 768], P(('regions', 'shard'))
- grad_up: float32 [768, 3072], P(('regions', 'shard'))
- firsts_up: float32 [768, 3072], P(('regions', 'shard'))
- seconds_up: float32 [768, 3072], P(('regions', 'shard'))
- update_up: float32 [768, 3072], P(('regions', 'shard'))
- grad_down: float32 [3072, 768], P(('regions', 'shard'))
- firsts_down: float32 [3072, 768], P(('regions', 'shard'))
- seconds_down: float32 [3072, 768], P(('regions', 'shard'))
- update_down: float32 [3072, 768], P(('regions', 'shard'))
- grad_vectors: float32 [12, 768], P(None, ('regions', 'shard'))
- firsts_vectors: float32 [12, 768], P(None, ('regions', 'shard'))
- seconds_vectors: float32 [12, 768], P(None, ('regions', 'shard'))
- update_vectors: float32 [12, 768], P(None, ('regions', 'shard'))
- grad_relative: float32 [12, 253], replicated
- firsts_relative: float32 [12, 253], replicated
- seconds_relative: float32 [12, 253], replicated
- update_relative: float32 [12, 253], replicated
Inputs may be any that keep to these rules, and one draw needn't show every extreme that they name: `token_slot`: in each replica, one device's entries are distinct; entry h * 72 + c means the c-th row that the device sends to device h, and the rows sent to h use slots 0 upward without gaps. Each device sends exactly 576 rows in all, at most 72 to one device, and exactly 72 to some device. `home_index`: in each replica, one device's entries are distinct and name exactly the rows sent to it: s * 72 + c is the c-th row from device s. Each device receives exactly 576 rows, at most 72 from one device, and exactly 72 from some device.
All inputs are finite; a program needn't handle non-finite values.
Results may differ from a plain program's by a relative error of at most 0.014.
The roundings to bfloat16 on the way count: a program that leaves them out, or rounds other values in their place, can miss the bound.
Values may be sent and summed in bfloat16 or wider, within the bound.
A program may use at most 192 MiB of HBM per device.

v0:
```python
import jax
import jax.numpy as jnp
import numpy as np
from jax import lax
from jax.sharding import PartitionSpec as P

HEADS = 12
HEAD = 64
PAGE = 576


PRECISE = lax.Precision.HIGHEST
EPS_NORM = 1e-05
BETA_ONE = 0.9
BETA_TWO = 0.999
ADAM_EPS = 1e-08
LAYER_FACTOR = 0.5625
DECAY_RATE = 0.05
STEP_COUNT = 10.0


def table_index():
    first_ax = np.arange(128)[:, None]
    second_ax = np.arange(128)[None, :]
    offset = second_ax - first_ax
    result = np.full((128, 128), -1)
    result = np.where((first_ax < 64) & (second_ax < 64), offset + 63, result)
    inside_x = (first_ax >= 64) & (first_ax < 96) & (second_ax >= 64) & (second_ax < 96)
    result = np.where(inside_x, offset + 158, result)
    result = np.where((first_ax >= 96) & (second_ax >= 96), offset + 221, result)
    return result


def bias_table(relative):
    indices = table_index()
    picked = relative[:, np.maximum(indices, 0)]
    return jnp.where(jnp.asarray(indices >= 0)[None], picked, jnp.zeros_like(picked))


def position_codes(box_x, box_y):
    places = jnp.arange(PAGE, dtype=jnp.int32)
    seq_bucket = places * 64 // PAGE
    columns = jnp.arange(128, dtype=jnp.int32)
    matched = (
        (columns[None, None, :] == seq_bucket[None, :, None])
        | (columns == 64 + box_x[..., None])
        | (columns == 96 + box_y[..., None])
    )
    return matched.astype(jnp.float32)


def layout_bias(code_rows, bias_mats):
    lifted = jnp.einsum("pa,hab->hpb", code_rows, bias_mats, precision=PRECISE)
    return jnp.einsum("hpb,qb->hpq", lifted, code_rows, precision=PRECISE)


def page_scores(page_qkv, code_rows, bias_mats):
    parted = page_qkv.reshape(PAGE, 3, HEADS, HEAD)
    queries = parted[:, 0]
    key_rows = parted[:, 1]
    values = parted[:, 2]
    scores = jnp.einsum(
        "phd,qhd->hpq", queries, key_rows, preferred_element_type=jnp.float32
    ) * 0.125 + layout_bias(code_rows, bias_mats)
    return (queries, key_rows, values, scores)


def page_forward(page_qkv, code_rows, bias_mats):
    queries, key_rows, values, scores = page_scores(page_qkv, code_rows, bias_mats)
    row_max = jnp.max(scores, axis=2, keepdims=True)
    raised = jnp.exp(scores - row_max)
    totals = jnp.sum(raised, axis=2, keepdims=True)
    attn_w = (raised / totals).astype(jnp.bfloat16)
    context = jnp.einsum("hpq,qhd->phd", attn_w, values, preferred_element_type=jnp.float32)
    log_total = (row_max + jnp.log(totals))[..., 0]
    return (context.reshape(PAGE, HEADS * HEAD).astype(jnp.bfloat16), log_total)


def page_backward(page_qkv, code_rows, log_total, grad_ctx, bias_mats):
    queries, key_rows, values, scores = page_scores(page_qkv, code_rows, bias_mats)
    chances = jnp.exp(scores - log_total[..., None])
    attn_w = chances.astype(jnp.bfloat16)
    grad_heads = grad_ctx.reshape(PAGE, HEADS, HEAD)
    grad_values = jnp.einsum("hpq,phd->qhd", attn_w, grad_heads, preferred_element_type=jnp.float32)
    grad_chances = jnp.einsum(
        "phd,qhd->hpq", grad_heads, values, preferred_element_type=jnp.float32
    )
    inner = jnp.sum(chances * grad_chances, axis=2, keepdims=True)
    grad_scores = (chances * (grad_chances - inner)).astype(jnp.bfloat16)
    grad_queries = (
        jnp.einsum("hpq,qhd->phd", grad_scores, key_rows, preferred_element_type=jnp.float32)
        * 0.125
    )
    grad_keys = (
        jnp.einsum("hpq,phd->qhd", grad_scores, queries, preferred_element_type=jnp.float32) * 0.125
    )
    partial_codes = jnp.einsum(
        "hpq,qb->hpb",
        grad_scores,
        code_rows.astype(jnp.bfloat16),
        preferred_element_type=jnp.float32,
    )
    grad_mats = jnp.einsum("pa,hpb->hab", code_rows, partial_codes, precision=PRECISE)
    grad_page = jnp.stack([grad_queries, grad_keys, grad_values], axis=1).reshape(
        PAGE, 3 * HEADS * HEAD
    )
    return (grad_page.astype(jnp.bfloat16), grad_mats)


def pack_rows(rows, targets, groups, slot_cap):
    buffer = jnp.zeros((groups * slot_cap, rows.shape[1]), rows.dtype).at[targets].set(rows)
    return buffer.reshape(groups, slot_cap, rows.shape[1])


def unpack_rows(arrived, picks):
    return arrived.reshape(-1, arrived.shape[2])[picks]


def norm_forward(rows, gain, shift):
    centre = rows - jnp.mean(rows, axis=-1, keepdims=True)
    spread = lax.rsqrt(jnp.mean(centre * centre, axis=-1, keepdims=True) + EPS_NORM)
    normed = centre * spread
    return (normed * gain + shift, normed, spread)


def norm_back(incoming, normed, spread, gain):
    scaled = incoming * gain
    grad_rows = spread * (
        scaled
        - jnp.mean(scaled, axis=-1, keepdims=True)
        - normed * jnp.mean(scaled * normed, axis=-1, keepdims=True)
    )
    return (grad_rows, jnp.sum(incoming * normed, axis=0), jnp.sum(incoming, axis=0))


def adam_step(param, grad, moment, square, decay):
    moment_new = BETA_ONE * moment + (1.0 - BETA_ONE) * grad
    square_new = BETA_TWO * square + (1.0 - BETA_TWO) * grad * grad
    moment_hat = moment_new / (1.0 - BETA_ONE**STEP_COUNT)
    square_hat = square_new / (1.0 - BETA_TWO**STEP_COUNT)
    update = LAYER_FACTOR * (moment_hat / (jnp.sqrt(square_hat) + ADAM_EPS) + decay * param)
    return (moment_new, square_new, update)


def per_device(
    layer_in,
    out_grad,
    w_qkv,
    w_out,
    w_up,
    w_down,
    vectors,
    relative,
    first_qkv,
    second_qkv,
    first_out,
    second_out,
    first_up,
    second_up,
    first_down,
    second_down,
    first_vectors,
    second_vectors,
    first_relative,
    second_relative,
    token_slot,
    home_index,
    box_x,
    box_y,
):
    tokens = layer_in[0]
    rows_dev = tokens.shape[0]
    model_dim = tokens.shape[1]
    groups = lax.axis_size("regions")
    slot_cap = 2 * rows_dev // groups
    page_num = rows_dev // PAGE
    slot_of = token_slot[0]
    home_rows = home_index[0]
    full_qkv, full_out, full_up, full_down, full_vec = (
        lax.all_gather(w_qkv, ("regions", "shard"), axis=0, tiled=True),
        lax.all_gather(w_out, ("regions", "shard"), axis=0, tiled=True),
        lax.all_gather(w_up, ("regions", "shard"), axis=0, tiled=True),
        lax.all_gather(w_down, ("regions", "shard"), axis=0, tiled=True),
        lax.all_gather(vectors, ("regions", "shard"), axis=1, tiled=True),
    )
    vec_rows = full_vec.astype(jnp.float32)
    qkv_bias = jnp.concatenate([vec_rows[0], jnp.zeros_like(vec_rows[0]), vec_rows[1]])
    code_rows = position_codes(box_x[0].reshape(page_num, PAGE), box_y[0].reshape(page_num, PAGE))
    bias_mats = bias_table(relative)
    projected = (jnp.dot(tokens, full_qkv, preferred_element_type=jnp.float32) + qkv_bias).astype(
        jnp.bfloat16
    )
    arrived = lax.all_to_all(
        pack_rows(projected, slot_of, groups, slot_cap),
        "regions",
        split_axis=0,
        concat_axis=0,
        tiled=True,
    )
    home_qkv = unpack_rows(arrived, home_rows)
    paged = home_qkv.reshape(page_num, PAGE, 3 * model_dim)
    context_pages, log_totals = lax.map(
        lambda member: page_forward(member[0], member[1], bias_mats), (paged, code_rows)
    )
    context_home = context_pages.reshape(rows_dev, model_dim)
    returned = lax.all_to_all(
        pack_rows(context_home, home_rows, groups, slot_cap),
        "regions",
        split_axis=0,
        concat_axis=0,
        tiled=True,
    )
    context = unpack_rows(returned, slot_of)
    attn_out = jnp.dot(context, full_out, preferred_element_type=jnp.float32) + vec_rows[2]
    hidden, normed_one, spread_one = norm_forward(
        tokens.astype(jnp.float32) + attn_out, vec_rows[3], vec_rows[4]
    )
    hidden_low = hidden.astype(jnp.bfloat16)
    pre_act = jnp.dot(hidden_low, full_up, preferred_element_type=jnp.float32) + vec_rows[
        8:12
    ].reshape(-1)
    activated, gelu_back = jax.vjp(lambda value: jax.nn.gelu(value, approximate=False), pre_act)
    act_low = activated.astype(jnp.bfloat16)
    branch = jnp.dot(act_low, full_down, preferred_element_type=jnp.float32) + vec_rows[5]
    result, normed_two, spread_two = norm_forward(hidden + branch, vec_rows[6], vec_rows[7])
    grad_two, grad_gain_two, grad_shift_two = norm_back(
        out_grad[0].astype(jnp.float32), normed_two, spread_two, vec_rows[6]
    )
    grad_branch = grad_two.astype(jnp.bfloat16)
    grad_down = jnp.einsum("tf,td->fd", act_low, grad_branch, preferred_element_type=jnp.float32)
    grad_act = jnp.einsum("td,fd->tf", grad_branch, full_down, preferred_element_type=jnp.float32)
    grad_pre = gelu_back(grad_act)[0].astype(jnp.bfloat16)
    grad_up = jnp.einsum("td,tf->df", hidden_low, grad_pre, preferred_element_type=jnp.float32)
    grad_hidden = grad_two + jnp.einsum(
        "tf,df->td", grad_pre, full_up, preferred_element_type=jnp.float32
    )
    grad_one, grad_gain_one, grad_shift_one = norm_back(
        grad_hidden, normed_one, spread_one, vec_rows[3]
    )
    grad_attn = grad_one.astype(jnp.bfloat16)
    grad_out = jnp.einsum("td,te->de", context, grad_attn, preferred_element_type=jnp.float32)
    grad_context = jnp.einsum(
        "te,de->td", grad_attn, full_out, preferred_element_type=jnp.float32
    ).astype(jnp.bfloat16)
    grad_arrived = lax.all_to_all(
        pack_rows(grad_context, slot_of, groups, slot_cap),
        "regions",
        split_axis=0,
        concat_axis=0,
        tiled=True,
    )
    grad_home = unpack_rows(grad_arrived, home_rows).reshape(page_num, PAGE, model_dim)
    grad_pages, mats_pages = lax.map(
        lambda member: page_backward(member[0], member[1], member[2], member[3], bias_mats),
        (paged, code_rows, log_totals, grad_home),
    )
    grad_dense = grad_pages.reshape(rows_dev, 3 * model_dim)
    bias_sums = jnp.sum(grad_dense.astype(jnp.float32), axis=0)
    grad_back = lax.all_to_all(
        pack_rows(grad_dense, home_rows, groups, slot_cap),
        "regions",
        split_axis=0,
        concat_axis=0,
        tiled=True,
    )
    grad_proj = unpack_rows(grad_back, slot_of)
    grad_qkv = jnp.einsum("td,tf->df", tokens, grad_proj, preferred_element_type=jnp.float32)
    in_grad = grad_one + jnp.einsum(
        "tf,df->td", grad_proj, full_qkv, preferred_element_type=jnp.float32
    )
    grad_vec = jnp.concatenate(
        [
            jnp.stack(
                [
                    bias_sums[:model_dim],
                    bias_sums[2 * model_dim :],
                    jnp.sum(grad_attn.astype(jnp.float32), axis=0),
                    grad_gain_one,
                    grad_shift_one,
                    jnp.sum(grad_branch.astype(jnp.float32), axis=0),
                    grad_gain_two,
                    grad_shift_two,
                ]
            ),
            jnp.sum(grad_pre.astype(jnp.float32), axis=0).reshape(4, model_dim),
        ],
        axis=0,
    )
    grad_qkv, grad_out, grad_up, grad_down, grad_vectors = (
        lax.psum_scatter(grad_qkv, ("regions", "shard"), scatter_dimension=0, tiled=True),
        lax.psum_scatter(grad_out, ("regions", "shard"), scatter_dimension=0, tiled=True),
        lax.psum_scatter(grad_up, ("regions", "shard"), scatter_dimension=0, tiled=True),
        lax.psum_scatter(grad_down, ("regions", "shard"), scatter_dimension=0, tiled=True),
        lax.psum_scatter(grad_vec, ("regions", "shard"), scatter_dimension=1, tiled=True),
    )
    mats_total = jnp.sum(mats_pages, axis=0)
    table_back = jax.vjp(bias_table, relative)[1]
    grad_relative = lax.psum(table_back(mats_total)[0], ("regions", "shard"))
    firsts_qkv, seconds_qkv, update_qkv = adam_step(
        w_qkv.astype(jnp.float32), grad_qkv, first_qkv, second_qkv, DECAY_RATE
    )
    firsts_out, seconds_out, update_out = adam_step(
        w_out.astype(jnp.float32), grad_out, first_out, second_out, DECAY_RATE
    )
    firsts_up, seconds_up, update_up = adam_step(
        w_up.astype(jnp.float32), grad_up, first_up, second_up, DECAY_RATE
    )
    firsts_down, seconds_down, update_down = adam_step(
        w_down.astype(jnp.float32), grad_down, first_down, second_down, DECAY_RATE
    )
    firsts_vectors, seconds_vectors, update_vectors = adam_step(
        vectors.astype(jnp.float32), grad_vectors, first_vectors, second_vectors, 0.0
    )
    firsts_relative, seconds_relative, update_relative = adam_step(
        relative, grad_relative, first_relative, second_relative, 0.0
    )
    return (
        result.astype(jnp.bfloat16)[None],
        in_grad[None],
        grad_qkv,
        firsts_qkv,
        seconds_qkv,
        update_qkv,
        grad_out,
        firsts_out,
        seconds_out,
        update_out,
        grad_up,
        firsts_up,
        seconds_up,
        update_up,
        grad_down,
        firsts_down,
        seconds_down,
        update_down,
        grad_vectors,
        firsts_vectors,
        seconds_vectors,
        update_vectors,
        grad_relative,
        firsts_relative,
        seconds_relative,
        update_relative,
    )


def solution(mesh):
    return jax.shard_map(
        per_device,
        mesh=mesh,
        in_specs=(
            P("shard", "regions", None),
            P("shard", "regions", None),
            P(("regions", "shard"), None),
            P(("regions", "shard"), None),
            P(("regions", "shard"), None),
            P(("regions", "shard"), None),
            P(None, ("regions", "shard")),
            P(),
            P(("regions", "shard"), None),
            P(("regions", "shard"), None),
            P(("regions", "shard"), None),
            P(("regions", "shard"), None),
            P(("regions", "shard"), None),
            P(("regions", "shard"), None),
            P(("regions", "shard"), None),
            P(("regions", "shard"), None),
            P(None, ("regions", "shard")),
            P(None, ("regions", "shard")),
            P(),
            P(),
            P("shard", "regions"),
            P("shard", "regions"),
            P("shard", "regions"),
            P("shard", "regions"),
        ),
        out_specs=(
            P("shard", "regions", None),
            P("shard", "regions", None),
            P(("regions", "shard"), None),
            P(("regions", "shard"), None),
            P(("regions", "shard"), None),
            P(("regions", "shard"), None),
            P(("regions", "shard"), None),
            P(("regions", "shard"), None),
            P(("regions", "shard"), None),
            P(("regions", "shard"), None),
            P(("regions", "shard"), None),
            P(("regions", "shard"), None),
            P(("regions", "shard"), None),
            P(("regions", "shard"), None),
            P(("regions", "shard"), None),
            P(("regions", "shard"), None),
            P(("regions", "shard"), None),
            P(("regions", "shard"), None),
            P(None, ("regions", "shard")),
            P(None, ("regions", "shard")),
            P(None, ("regions", "shard")),
            P(None, ("regions", "shard")),
            P(),
            P(),
            P(),
            P(),
        ),
        check_vma=False,
    )
```

profile of v0, /device:TPU:0, one launch (start us, length us, event | category | flops | bytes accessed | tf_op | source)
XLA Modules:
  0.0 964.3 jit_solution(7731919277228249692)
XLA Ops:
  9.4 44.1 %all-gather = bf16[32,24,12]{1,2,0:T(8,128)(2,1)S(1)} all-gather(bf16[1,24,12]{1,2,0:T(8,128)(2,1)} %bitcast.165), channel_id=1, replica_groups=mesh['regions'=16,'shard'=2] {'regions','shard'}, dimensions={0}, use_global_device_ids=true | all-gather | bytes 19008 | tf_op jit(solution)/shard_map/all_gather | solution.py:184
  55.3 18.6 %all-gather.6.cloned.1.call-done = bf16[768,2304]{1,0:T(8,128)(2,1)} async-done(((bf16[24,2304]{1,0:T(8,128)(2,1)}), bf16[768,2304]{1,0:T(8,128)(2,1)}) %all-gather.6.cloned.1.call-update) | async-done | bytes 3538960 | tf_op jit(solution)/shard_map/all_gather | solution.py:180
  73.9 4.5 add_convert_fusion.1
  78.4 10.7 %scatter_custom_fusion = bf16[1152,2304]{1,0:T(8,128)(2,1)} fusion(s32[576]{0:T(1024)S(1)} %fusion.65, bf16[576,2304]{1,0:T(8,128)(2,1)S(1)} %add_convert_fusion.1, bf16[]{:T(256)} %constant.56.clone.1), kind=kCustom, calls=%fused_computation.47 | custom fusion | bytes 5308418 | tf_op jit(solution)/shard_map/scatter | solution.py:111
  89.2 4.7 all-to-all-start
  94.6 54.4 %gather_fusion.1 = f32[16384,12]{1,0:T(8,128)} fusion(f32[12,253]{0,1:T(8,128)S(1)} %copy.148, s32[16384]{0:T(1024)S(1)} %broadcast_clamp_fusion), kind=kCustom, calls=%fused_computation.1 | custom fusion | bytes 1638400 | tf_op jit(solution)/shard_map/gather | solution.py:36
  149.1 5.5 copy.149
  156.4 11.0 %fusion.12 = f32[12,576,576]{1,2,0:T(8,128)} fusion(f32[12,128,576]{1,2,0:T(8,128)S(1)} %fusion.42, s32[576]{0:T(1024)S(1)} %get-tuple-element.231, s32[576]{0:T(1024)S(1)} %get-tuple-element.232, s32[576]{0:T(1024)S(1)} %add_select_fusion), kind=kOutput, calls=%fused_computation.43 | convolution fusion | flops 6115663872 | bytes 19471104 | tf_op jit(solution)/shard_map/while/body/eval_jaxpr/hpb,qb->hpq/dot_general | solution.py:54
  167.4 32.4 %all-to-all-done = bf16[16,72,2304]{2,1,0:T(8,128)(2,1)} async-done(((bf16[16,72,2304]{2,1,0:T(8,128)(2,1)}), bf16[16,72,2304]{2,1,0:T(8,128)(2,1)}, u32[]{:S(2)}, u32[]{:S(2)}) %all-to-all-start) | async-done | bytes 5308448 | tf_op jit(solution)/shard_map/all_to_all | solution.py:193
  199.8 10.8 %gather_fusion = bf16[576,2304]{1,0:T(8,128)(2,1)} fusion(bf16[1152,2304]{1,0:T(8,128)(2,1)} %bitcast.7, s32[1024]{0:T(1024)S(1)} %pad_clamp_fusion.1), kind=kCustom, calls=%fused_computation | custom fusion | bytes 5310720 | tf_op jit(solution)/shard_map/gather | solution.py:116
  210.6 4.0 copy.146
  214.6 12.7 %fusion.93 = (f32[12,576]{1,0:T(8,128)S(1)}, f32[12,576,576]{1,2,0:T(8,128)}) fusion(f32[12,576,576]{1,2,0:T(8,128)} %fusion.12, bf16[576,3,12,64]{0,3,2,1:T(8,128)(2,1)S(1)} %bitcast.147), kind=kOutput, calls=%fused_computation.182 | convolution fusion | flops 521544960 | bytes 33844224 | tf_op jit(solution)/shard_map/while/body/eval_jaxpr/phd,qhd->hpq/dot_general | solution.py:62
  227.3 8.5 fusion
  235.9 10.3 %fusion.31 = bf16[12,64,576]{2,1,0:T(8,128)(2,1)} fusion(f32[12,576,576]{1,2,0:T(8,128)} %get-tuple-element.220, f32[12,576]{1,0:T(8,128)S(1)} %fusion, f32[12,576]{1,0:T(8,128)S(1)} %get-tuple-element.219, bf16[576,3,12,64]{0,3,2,1:T(8,128)(2,1)S(1)} %bitcast.148), kind=kOutput, calls=%fused_computation.79 | convolution fusion | flops 521994240 | bytes 17874944 | tf_op jit(solution)/shard_map/while/body/eval_jaxpr/hpq,qhd->phd/dot_general | solution.py:74
  247.7 7.0 scatter_custom_fusion.1
  254.7 28.7 %all-to-all-start.1 = ((bf16[16,72,768]{2,1,0:T(8,128)(2,1)}), bf16[16,72,768]{2,1,0:T(8,128)(2,1)S(1)}, u32[]{:S(2)}, u32[]{:S(2)}) async-start(bf16[16,72,768]{2,1,0:T(8,128)(2,1)} %bitcast.18), calls=%async_computation.1 | async-start | bytes 3538944 | tf_op jit(solution)/shard_map/all_to_all | solution.py:206
  284.2 42.3 %all-to-all-done.1 = bf16[16,72,768]{2,1,0:T(8,128)(2,1)S(1)} async-done(((bf16[16,72,768]{2,1,0:T(8,128)(2,1)}), bf16[16,72,768]{2,1,0:T(8,128)(2,1)S(1)}, u32[]{:S(2)}, u32[]{:S(2)}) %all-to-all-start.1) | async-done | bytes 1769504 | tf_op jit(solution)/shard_map/all_to_all | solution.py:206
  326.5 3.5 gather_fusion.2
  330.0 2.8 fusion.94
  333.2 21.8 %multiply_convert_fusion.1 = (bf16[576,3072]{1,0:T(8,128)(2,1)}, f32[576,3072]{1,0:T(8,128)}, f32[576,3072]{1,0:T(8,128)}) fusion(f32[3072]{0:T(1024)S(1)} %copy-done.42, bf16[768,3072]{1,0:T(8,128)(2,1)} %all-gather.10.cloned.1.call-done, f32[576,768]{1,0:T(8,128)S(1)} %get-tuple-element.222, f32[768]{0:T(1024)S(1)} %get-tuple-element.182, ...), kind=kOutput, calls=%fused_computation.25 | convolution fusion | flops 2836905984 | bytes 24205824 | tf_op jit(solution)/shard_map/dot_general | solution.py:219
  355.0 6.6 fusion.95
  365.6 9.3 convert_reduce_fusion
  374.9 3.9 multiply_reduce_fusion.1
  381.3 2.5 fusion.66
  383.9 8.8 fusion.69
  394.2 3.1 convolution_convert_fusion
  397.2 7.6 scatter_custom_fusion.2
  404.8 18.7 %all-to-all-start.2 = ((bf16[16,72,768]{2,1,0:T(8,128)(2,1)}), bf16[16,72,768]{2,1,0:T(8,128)(2,1)S(1)}, u32[]{:S(2)}, u32[]{:S(2)}) async-start(bf16[16,72,768]{2,1,0:T(8,128)(2,1)} %bitcast.159), calls=%async_computation.2 | async-start | bytes 3538944 | tf_op jit(solution)/shard_map/all_to_all | solution.py:245
  425.1 8.6 fusion.80
  433.7 28.9 %all-to-all-done.2 = bf16[16,72,768]{2,1,0:T(8,128)(2,1)S(1)} async-done(((bf16[16,72,768]{2,1,0:T(8,128)(2,1)}), bf16[16,72,768]{2,1,0:T(8,128)(2,1)S(1)}, u32[]{:S(2)}, u32[]{:S(2)}) %all-to-all-start.2) | async-done | bytes 1769504 | tf_op jit(solution)/shard_map/all_to_all | solution.py:245
  462.6 3.1 gather_fusion.3
  466.4 11.7 %multiply_reduce_fusion = (f32[12,576]{1,0:T(8,128)S(1)}, f32[12,576,576]{1,2,0:T(8,128)}) fusion(f32[12,576,576]{1,2,0:T(8,128)} %get-tuple-element.220, f32[12,576]{1,0:T(8,128)S(1)} %copy-done.9, bf16[576,12,64]{0,2,1:T(8,128)(2,1)S(1)} %bitcast.156, bf16[576,3,12,64]{0,3,2,1:T(8,128)(2,1)} %bitcast.149), kind=kOutput, calls=%fused_computation.11 | convolution fusion | flops 521544960 | bytes 35543040 | tf_op jit(solution)/shard_map/while/body/eval_jaxpr/phd,qhd->hpq/dot_general | solution.py:85
  478.1 12.5 %multiply_convert_fusion = bf16[12,576,576]{1,2,0:T(8,128)(2,1)S(1)} fusion(f32[12,576,576]{1,2,0:T(8,128)} %get-tuple-element.228, f32[12,576,576]{1,2,0:T(8,128)} %get-tuple-element.220, f32[12,576]{1,0:T(8,128)S(1)} %get-tuple-element.227, f32[12,576]{1,0:T(8,128)S(1)} %copy-done.9), kind=kLoop, calls=%fused_computation.10 | loop fusion | flops 15925248 | bytes 39868416 | tf_op jit(solution)/shard_map/while/body/eval_jaxpr/convert_element_type | solution.py:89
  490.6 2.7 multiply_bitcast_fusion
  495.8 8.8 fusion.27
  505.9 3.5 copy.156
  509.4 12.1 %scatter_custom_fusion.3 = bf16[1152,2304]{1,0:T(8,128)(2,1)} fusion(s32[576]{0:T(1024)} %copy-done.36, bf16[576,2304]{1,0:T(8,128)(2,1)} %copy.156, bf16[]{:T(256)} %constant.56.clone.1), kind=kCustom, calls=%fused_computation.45 | custom fusion | bytes 5308928 | tf_op jit(solution)/shard_map/scatter | solution.py:111
  521.4 172.3 %all_to_all.20 = bf16[16,72,2304]{2,1,0:T(8,128)(2,1)} all-to-all(bf16[16,72,2304]{2,1,0:T(8,128)(2,1)} %bitcast.153), channel_id=1, replica_groups=mesh['regions'=16,'shard'=2] {'regions'}, dimensions={0} | all-to-all | bytes 10616832 | tf_op jit(solution)/shard_map/all_to_all | solution.py:259
  693.7 10.2 %gather_fusion.4 = bf16[576,2304]{1,0:T(8,128)(2,1)S(1)} fusion(bf16[1152,2304]{1,0:T(8,128)(2,1)} %bitcast.144, s32[1024]{0:T(1024)S(1)} %copy-done.27), kind=kCustom, calls=%fused_computation.4 | custom fusion | bytes 5310720 | tf_op jit(solution)/shard_map/gather | solution.py:116
  703.9 6.2 convolution_bitcast_fusion
  710.2 8.3 copy.172
  727.7 7.0 fusion.56
  734.7 3.6 fusion.33
  738.4 7.9 copy.171
  746.3 100.9 %scatter_custom_fusion.4 = f32[12,253]{0,1:T(8,128)S(1)} fusion(s32[16384]{0:T(1024)} %constant.133, f32[16384,12]{1,0:T(8,128)} %bitcast.158, f32[]{:T(128)} %constant.59.clone.1), kind=kCustom, calls=%fused_computation.128 | custom fusion | flops 196608 | bytes 12656 | tf_op jit(solution)/shard_map/transpose(jvp())/scatter-add | solution.py:36
  847.4 38.9 %all-reduce.1 = (f32[12,768]{1,0:T(8,128)S(1)}, f32[12,253]{1,0:T(8,128)S(1)}) all-reduce(f32[12,768]{1,0:T(8,128)S(1)} %concatenate.7, f32[12,253]{1,0:T(8,128)S(1)} %copy.164), channel_id=6, replica_groups=mesh['regions'=16,'shard'=2] {'regions','shard'}, use_global_device_ids=true, to_apply=%region_27.28.clone | all-reduce | flops 12252 | bytes 98016
  892.9 6.1 add_bitcast_fusion
  898.9 56.2 %reduce-scatter.14.cloned.1.call-done = f32[24,2304]{1,0:T(8,128)} async-done(((f32[768,2304]{1,0:T(8,128)}), f32[24,2304]{1,0:T(8,128)}) %reduce-scatter.14.cloned.1.call-update) | async-done | bytes 221200
  (179 shorter events, 40.7 us)
Async XLA Ops:
  7.2 66.7 %all-gather.6.cloned.1.call-start = ((), (), s32[]{:S(2)}) async-start(), calls=%async_computation.8 | async-start | bytes 3649536 | tf_op jit(solution)/shard_map/all_gather | solution.py:180
  7.9 322.0 %all-gather.8.cloned.1.call-start = ((), (), s32[]{:S(2)}) async-start(), calls=%async_computation.9 | async-start | bytes 1216512 | tf_op jit(solution)/shard_map/all_gather | solution.py:181
  8.7 324.5 %all-gather.10.cloned.1.call-start = ((), (), s32[]{:S(2)}) async-start(), calls=%async_computation.10 | async-start | bytes 4866048 | tf_op jit(solution)/shard_map/all_gather | solution.py:182
  55.3 228.9 %copy-start.37 = (s32[576]{0:T(1024)}, s32[576]{0:T(1024)S(1)}, u32[]{:S(2)}) copy-start(s32[576]{0:T(1024)S(1)} %fusion.65) | copy-start | bytes 6916
  89.2 110.7 %all-to-all-start = ((bf16[16,72,2304]{2,1,0:T(8,128)(2,1)}), bf16[16,72,2304]{2,1,0:T(8,128)(2,1)}, u32[]{:S(2)}, u32[]{:S(2)}) async-start(bf16[16,72,2304]{2,1,0:T(8,128)(2,1)} %bitcast.152), calls=%async_computation | async-start | bytes 10616832 | tf_op jit(solution)/shard_map/all_to_all | solution.py:193
  93.9 261.1 %all-gather.12.cloned.1.call-start = ((), (), s32[]{:S(2)}) async-start(), calls=%async_computation.11 | async-start | bytes 4866048 | tf_op jit(solution)/shard_map/all_gather | solution.py:183
  149.0 5.5 copy-start.45
  149.0 5.6 copy-start.46
  149.0 5.6 copy-start.47
  149.0 5.7 copy-start.30
  154.6 12.8 %copy-start.15 = (s32[576]{0:T(1024)}, s32[576]{0:T(1024)S(1)}, u32[]{:S(2)}) copy-start(s32[576]{0:T(1024)S(1)} %add_select_fusion) | copy-start | bytes 6916
  154.6 93.1 %copy-start.36 = (s32[576]{0:T(1024)}, s32[576]{0:T(1024)S(1)}, u32[]{:S(2)}) copy-start(s32[576]{0:T(1024)S(1)} %fusion.64) | copy-start | bytes 6916
  154.7 45.2 %copy-start.24 = (s32[1024]{0:T(1024)}, s32[1024]{0:T(1024)S(1)}, u32[]{:S(2)}) copy-start(s32[1024]{0:T(1024)S(1)} %pad_clamp_fusion.1) | copy-start | bytes 12292
  154.7 12.7 %copy-start.17 = (s32[576]{0:T(1024)}, s32[576]{0:T(1024)S(1)}, u32[]{:S(2)}) copy-start(s32[576]{0:T(1024)S(1)} %get-tuple-element.231) | copy-start | bytes 6916
  154.7 12.7 %copy-start.19 = (s32[576]{0:T(1024)}, s32[576]{0:T(1024)S(1)}, u32[]{:S(2)}) copy-start(s32[576]{0:T(1024)S(1)} %get-tuple-element.232) | copy-start | bytes 6916
  214.6 21.2 %copy-start.1 = (bf16[576,2304]{0,1:T(8,128)(2,1)}, bf16[576,2304]{0,1:T(8,128)(2,1)S(1)}, u32[]{:S(2)}) copy-start(bf16[576,2304]{0,1:T(8,128)(2,1)S(1)} %copy.146) | copy-start | bytes 7962628
  227.3 8.6 copy-start.11
  235.9 10.3 %copy-start.14 = (f32[12,576]{1,0:T(8,128)}, f32[12,576]{1,0:T(8,128)S(1)}, u32[]{:S(2)}) copy-start(f32[12,576]{1,0:T(8,128)S(1)} %fusion) | copy-start | bytes 82948
  254.7 71.8 %all-to-all-start.1 = ((bf16[16,72,768]{2,1,0:T(8,128)(2,1)}), bf16[16,72,768]{2,1,0:T(8,128)(2,1)S(1)}, u32[]{:S(2)}, u32[]{:S(2)}) async-start(bf16[16,72,768]{2,1,0:T(8,128)(2,1)} %bitcast.18), calls=%async_computation.1 | async-start | bytes 3538944 | tf_op jit(solution)/shard_map/all_to_all | solution.py:206
  283.5 440.5 %reduce-scatter.8.cloned.1.call-start = ((), (), s32[]{:S(2)}) async-start(), calls=%async_computation.12 | async-start | bytes 2433024 | tf_op jit(solution)/shard_map/reduce_scatter | solution.py:291
  284.2 45.8 %copy-start.26 = (s32[1024]{0:T(1024)}, s32[1024]{0:T(1024)S(1)}, u32[]{:S(2)}) copy-start(s32[1024]{0:T(1024)S(1)} %pad_clamp_fusion) | copy-start | bytes 12292
  333.2 21.8 %copy-start.44 = (f32[768]{0:T(1024)S(1)}, f32[768]{0:T(1024)}, u32[]{:S(2)}) copy-start(f32[768]{0:T(1024)} %get-tuple-element.181) | copy-start | bytes 9220
  355.0 7.0 copy-start.3
  355.0 7.0 copy-start.28
  363.4 11.5 %slice-start = ((s8[4718592]{0:T(1024)(128)(4,1)}), s8[4194304]{0:T(1024)(128)(4,1)S(1)}, s32[]{:S(2)}) async-start(s8[4718592]{0:T(1024)(128)(4,1)} %bitcast.166), calls=%async_computation.16 | async-start | bytes 8388608
  365.6 9.3 slice-start.1
  383.8 504.5 %reduce-scatter.12.cloned.1.call-start = ((), (), s32[]{:S(2)}) async-start(), calls=%async_computation.14 | async-start | bytes 9732096 | tf_op jit(solution)/shard_map/reduce_scatter | solution.py:293
  404.8 57.8 %all-to-all-start.2 = ((bf16[16,72,768]{2,1,0:T(8,128)(2,1)}), bf16[16,72,768]{2,1,0:T(8,128)(2,1)S(1)}, u32[]{:S(2)}, u32[]{:S(2)}) async-start(bf16[16,72,768]{2,1,0:T(8,128)(2,1)} %bitcast.159), calls=%async_computation.2 | async-start | bytes 3538944 | tf_op jit(solution)/shard_map/all_to_all | solution.py:245
  423.6 467.0 %reduce-scatter.10.cloned.1.call-start = ((), (), s32[]{:S(2)}) async-start(), calls=%async_computation.13 | async-start | bytes 9732096 | tf_op jit(solution)/shard_map/reduce_scatter | solution.py:292
  433.6 29.0 %copy-start.25 = (s32[1024]{0:T(1024)S(1)}, s32[1024]{0:T(1024)}, u32[]{:S(2)}) copy-start(s32[1024]{0:T(1024)} %copy-done.24) | copy-start | bytes 12292
  433.7 521.4 %reduce-scatter.14.cloned.1.call-start = ((), (), s32[]{:S(2)}) async-start(), calls=%async_computation.15 | async-start | bytes 7299072
  478.1 12.5 %copy-start.2 = (bf16[576,2304]{0,1:T(8,128)(2,1)S(1)}, bf16[576,2304]{0,1:T(8,128)(2,1)}, u32[]{:S(2)}) copy-start(bf16[576,2304]{0,1:T(8,128)(2,1)} %copy-done.1) | copy-start | bytes 7962628
  521.4 172.3 %copy-start.27 = (s32[1024]{0:T(1024)S(1)}, s32[1024]{0:T(1024)}, u32[]{:S(2)}) copy-start(s32[1024]{0:T(1024)} %copy-done.26) | copy-start | bytes 12292
  718.5 9.2 copy-start.16
  718.5 9.2 copy-start.18
  718.5 9.2 copy-start.20
  727.7 7.0 copy-start.29
  738.3 108.9 %copy-start.39 = (f32[1,768]{1,0:T(1,128)S(1)}, f32[1,768]{1,0:T(1,128)}, u32[]{:S(2)}) copy-start(f32[1,768]{1,0:T(1,128)} %stack.46) | copy-start | bytes 9220
  738.3 108.9 %copy-start.40 = (f32[1,768]{1,0:T(1,128)S(1)}, f32[1,768]{1,0:T(1,128)}, u32[]{:S(2)}) copy-start(f32[1,768]{1,0:T(1,128)} %stack.45) | copy-start | bytes 9220
  738.4 108.9 %copy-start.41 = (f32[1,768]{1,0:T(1,128)S(1)}, f32[1,768]{1,0:T(1,128)}, u32[]{:S(2)}) copy-start(f32[1,768]{1,0:T(1,128)} %stack.44) | copy-start | bytes 9220
  738.4 147.9 %copy-start.38 = (bf16[12,24]{1,0:T(8,128)(2,1)S(1)}, bf16[12,24]{1,0:T(8,128)(2,1)}, u32[]{:S(2)}) copy-start(bf16[12,24]{1,0:T(8,128)(2,1)} %param.36) | copy-start | bytes 1732
  738.4 149.3 %copy-start.22 = (f32[12,253]{1,0:T(8,128)S(1)}, f32[12,253]{1,0:T(8,128)}, u32[]{:S(2)}) copy-start(f32[12,253]{1,0:T(8,128)} %param.37) | copy-start | bytes 36436
  738.4 149.3 %copy-start.33 = (f32[12,253]{1,0:T(8,128)S(1)}, f32[12,253]{1,0:T(8,128)}, u32[]{:S(2)}) copy-start(f32[12,253]{1,0:T(8,128)} %param.49) | copy-start | bytes 36436
  738.4 149.3 %copy-start.34 = (f32[12,253]{1,0:T(8,128)S(1)}, f32[12,253]{1,0:T(8,128)}, u32[]{:S(2)}) copy-start(f32[12,253]{1,0:T(8,128)} %param.48) | copy-start | bytes 36436
  886.2 12.7 %copy-start.35 = (f32[12,253]{1,0:T(8,128)}, f32[12,253]{1,0:T(8,128)S(1)}, u32[]{:S(2)}) copy-start(f32[12,253]{1,0:T(8,128)S(1)} %get-tuple-element.188) | copy-start | bytes 36436
  892.9 62.3 %copy-start.10 = (bf16[24,2304]{1,0:T(8,128)(2,1)S(1)}, bf16[24,2304]{1,0:T(8,128)(2,1)}, u32[]{:S(2)}) copy-start(bf16[24,2304]{1,0:T(8,128)(2,1)} %param.32) | copy-start | bytes 331780
  892.9 62.3 %copy-start.12 = (f32[24,2304]{1,0:T(8,128)S(1)}, f32[24,2304]{1,0:T(8,128)}, u32[]{:S(2)}) copy-start(f32[24,2304]{1,0:T(8,128)} %param.39) | copy-start | bytes 663556
  892.9 62.3 %copy-start.13 = (f32[24,2304]{1,0:T(8,128)S(1)}, f32[24,2304]{1,0:T(8,128)}, u32[]{:S(2)}) copy-start(f32[24,2304]{1,0:T(8,128)} %param.38) | copy-start | bytes 663556
  (14 other events, 41.9 us)
Sparse Core Ops, SparseCore 0:
  10.9 62.9 all-gather.5
  76.8 101.1 all-gather.7
  180.9 84.0 all-gather.9
  267.7 77.6 all-gather.11
  383.9 118.1 reduce-scatter.7
  509.5 178.6 reduce-scatter.11
  694.6 135.1 reduce-scatter.9
  837.1 118.0 reduce-scatter.13
where the time goes:
time: 973 us; the launch traced here: 964 us
  blocking collectives  255 us (26%)
  waiting for transfers between devices  181 us (19%)
  local copies, waits for them, and re-layouts  164 us (17%)
  matrix products  155 us (16%)
  other arithmetic  141 us (14%)
  starting transfers between devices  52.7 us (5%)
  between operations  15.3 us (2%)
    all_to_all x1, blocking collectives, per_device(): lax.all_to_all(pack_rows(grad_dense, home_rows, groups, slot_cap), 'regio...  172 us
    scatter-add x1, other arithmetic, bias_table(): picked = relative[:, np.maximum(indices, 0)]  101 us
    gather x2, local copies, waits for them, and re-layouts, bias_table(): picked = relative[:, np.maximum(indices, 0)]  59.9 us
    unnamed x9, waiting for transfers between devices  58.6 us
    all_gather x1, blocking collectives, per_device(): lax.all_gather(vectors, ('regions', 'shard'), axis=1, tiled=True)  44.1 us
    all_to_all x1, waiting for transfers between devices, per_device(): lax.all_to_all(pack_rows(context_home, home_rows, groups, slot_cap), 'reg...  42.3 us
    unnamed x1, blocking collectives  38.9 us
    scatter x4, local copies, waits for them, and re-layouts, pack_rows(): jnp.zeros((groups * slot_cap, rows.shape[1]), rows.dtype).at[targets]  37.4 us
  transfers between devices with their start and end apart: 11, of which 5 were waited for; matrix products, arithmetic and copies ran while one was open for 44% of the time, Pallas kernels for 0%

commit v1 on v0

--- a/solution.py
+++ b/solution.py
@@ -19,22 +19,23 @@
 STEP_COUNT = 10.0
 
 
-def table_index():
-    first_ax = np.arange(128)[:, None]
-    second_ax = np.arange(128)[None, :]
-    offset = second_ax - first_ax
-    result = np.full((128, 128), -1)
-    result = np.where((first_ax < 64) & (second_ax < 64), offset + 63, result)
-    inside_x = (first_ax >= 64) & (first_ax < 96) & (second_ax >= 64) & (second_ax < 96)
-    result = np.where(inside_x, offset + 158, result)
-    result = np.where((first_ax >= 96) & (second_ax >= 96), offset + 221, result)
-    return result
+def skewed(line, size):
+    count = line.shape[0]
+    wide = jnp.pad(line, ((0, 0), (0, 1)))
+    flat = jnp.broadcast_to(wide[:, None, :], (count, size, 2 * size)).reshape(count, -1)
+    rows = flat[:, : size * (2 * size - 1)].reshape(count, size, 2 * size - 1)
+    return rows[:, :, size - 1 :]
 
 
 def bias_table(relative):
-    indices = table_index()
-    picked = relative[:, np.maximum(indices, 0)]
-    return jnp.where(jnp.asarray(indices >= 0)[None], picked, jnp.zeros_like(picked))
+    seq = skewed(relative[:, :127], 64)
+    horizontal = skewed(relative[:, 127:190], 32)
+    vertical = skewed(relative[:, 190:253], 32)
+    return (
+        jnp.pad(seq, ((0, 0), (0, 64), (0, 64)))
+        + jnp.pad(horizontal, ((0, 0), (64, 32), (64, 32)))
+        + jnp.pad(vertical, ((0, 0), (96, 0), (96, 0)))
+    )
 
 
 def position_codes(box_x, box_y):
@@ -107,13 +108,20 @@
     return (grad_page.astype(jnp.bfloat16), grad_mats)
 
 
-def pack_rows(rows, targets, groups, slot_cap):
-    buffer = jnp.zeros((groups * slot_cap, rows.shape[1]), rows.dtype).at[targets].set(rows)
-    return buffer.reshape(groups, slot_cap, rows.shape[1])
-
-
-def unpack_rows(arrived, picks):
-    return arrived.reshape(-1, arrived.shape[2])[picks]
+def exchange(rows, targets, picks, groups, slot_cap):
+    slots = groups * slot_cap
+    places = jnp.arange(slots, dtype=jnp.int32)
+    packing = (places[:, None] == targets[None, :]).astype(jnp.bfloat16)
+    packed = jnp.dot(packing, rows, preferred_element_type=jnp.float32).astype(jnp.bfloat16)
+    arrived = lax.all_to_all(
+        packed.reshape(groups, slot_cap, rows.shape[1]),
+        "regions",
+        split_axis=0,
+        concat_axis=0,
+        tiled=True,
+    ).reshape(slots, rows.shape[1])
+    picking = (picks[:, None] == places[None, :]).astype(jnp.bfloat16)
+    return jnp.dot(picking, arrived, preferred_element_type=jnp.float32)
 
 
 def norm_forward(rows, gain, shift):
@@ -187,33 +195,19 @@
     qkv_bias = jnp.concatenate([vec_rows[0], jnp.zeros_like(vec_rows[0]), vec_rows[1]])
     code_rows = position_codes(box_x[0].reshape(page_num, PAGE), box_y[0].reshape(page_num, PAGE))
     bias_mats = bias_table(relative)
-    projected = (jnp.dot(tokens, full_qkv, preferred_element_type=jnp.float32) + qkv_bias).astype(
+    homed = exchange(tokens, slot_of, home_rows, groups, slot_cap).astype(jnp.bfloat16)
+    cotangent = exchange(out_grad[0], slot_of, home_rows, groups, slot_cap)
+    projected = (jnp.dot(homed, full_qkv, preferred_element_type=jnp.float32) + qkv_bias).astype(
         jnp.bfloat16
     )
-    arrived = lax.all_to_all(
-        pack_rows(projected, slot_of, groups, slot_cap),
-        "regions",
-        split_axis=0,
-        concat_axis=0,
-        tiled=True,
-    )
-    home_qkv = unpack_rows(arrived, home_rows)
-    paged = home_qkv.reshape(page_num, PAGE, 3 * model_dim)
+    paged = projected.reshape(page_num, PAGE, 3 * model_dim)
     context_pages, log_totals = lax.map(
         lambda member: page_forward(member[0], member[1], bias_mats), (paged, code_rows)
     )
-    context_home = context_pages.reshape(rows_dev, model_dim)
-    returned = lax.all_to_all(
-        pack_rows(context_home, home_rows, groups, slot_cap),
-        "regions",
-        split_axis=0,
-        concat_axis=0,
-        tiled=True,
-    )
-    context = unpack_rows(returned, slot_of)
+    context = context_pages.reshape(rows_dev, model_dim)
     attn_out = jnp.dot(context, full_out, preferred_element_type=jnp.float32) + vec_rows[2]
     hidden, normed_one, spread_one = norm_forward(
-        tokens.astype(jnp.float32) + attn_out, vec_rows[3], vec_rows[4]
+        homed.astype(jnp.float32) + attn_out, vec_rows[3], vec_rows[4]
     )
     hidden_low = hidden.astype(jnp.bfloat16)
     pre_act = jnp.dot(hidden_low, full_up, preferred_element_type=jnp.float32) + vec_rows[
@@ -224,7 +218,7 @@
     branch = jnp.dot(act_low, full_down, preferred_element_type=jnp.float32) + vec_rows[5]
     result, normed_two, spread_two = norm_forward(hidden + branch, vec_rows[6], vec_rows[7])
     grad_two, grad_gain_two, grad_shift_two = norm_back(
-        out_grad[0].astype(jnp.float32), normed_two, spread_two, vec_rows[6]
+        cotangent, normed_two, spread_two, vec_rows[6]
     )
     grad_branch = grad_two.astype(jnp.bfloat16)
     grad_down = jnp.einsum("tf,td->fd", act_low, grad_branch, preferred_element_type=jnp.float32)
@@ -242,32 +236,19 @@
     grad_context = jnp.einsum(
         "te,de->td", grad_attn, full_out, preferred_element_type=jnp.float32
     ).astype(jnp.bfloat16)
-    grad_arrived = lax.all_to_all(
-        pack_rows(grad_context, slot_of, groups, slot_cap),
-        "regions",
-        split_axis=0,
-        concat_axis=0,
-        tiled=True,
-    )
-    grad_home = unpack_rows(grad_arrived, home_rows).reshape(page_num, PAGE, model_dim)
+    grad_home = grad_context.reshape(page_num, PAGE, model_dim)
     grad_pages, mats_pages = lax.map(
         lambda member: page_backward(member[0], member[1], member[2], member[3], bias_mats),
         (paged, code_rows, log_totals, grad_home),
     )
     grad_dense = grad_pages.reshape(rows_dev, 3 * model_dim)
     bias_sums = jnp.sum(grad_dense.astype(jnp.float32), axis=0)
-    grad_back = lax.all_to_all(
-        pack_rows(grad_dense, home_rows, groups, slot_cap),
-        "regions",
-        split_axis=0,
-        concat_axis=0,
-        tiled=True,
-    )
-    grad_proj = unpack_rows(grad_back, slot_of)
-    grad_qkv = jnp.einsum("td,tf->df", tokens, grad_proj, preferred_element_type=jnp.float32)
-    in_grad = grad_one + jnp.einsum(
-        "tf,df->td", grad_proj, full_qkv, preferred_element_type=jnp.float32
-    )
+    grad_qkv = jnp.einsum("td,tf->df", homed, grad_dense, preferred_element_type=jnp.float32)
+    in_home = grad_one + jnp.einsum(
+        "tf,df->td", grad_dense, full_qkv, preferred_element_type=jnp.float32
+    )
+    layer_out = exchange(result.astype(jnp.bfloat16), home_rows, slot_of, groups, slot_cap)
+    in_grad = exchange(in_home.astype(jnp.bfloat16), home_rows, slot_of, groups, slot_cap)
     grad_vec = jnp.concatenate(
         [
             jnp.stack(
@@ -287,10 +268,10 @@
         axis=0,
     )
     grad_qkv, grad_out, grad_up, grad_down, grad_vectors = (
-        lax.psum_scatter(grad_qkv, ("regions", "shard"), scatter_dimension=0, tiled=True),
-        lax.psum_scatter(grad_out, ("regions", "shard"), scatter_dimension=0, tiled=True),
-        lax.psum_scatter(grad_up, ("regions", "shard"), scatter_dimension=0, tiled=True),
-        lax.psum_scatter(grad_down, ("regions", "shard"), scatter_dimension=0, tiled=True),
+        lax.psum_scatter(grad_qkv.astype(jnp.bfloat16), ("regions", "shard"), scatter_dimension=0, tiled=True).astype(jnp.float32),
+        lax.psum_scatter(grad_out.astype(jnp.bfloat16), ("regions", "shard"), scatter_dimension=0, tiled=True).astype(jnp.float32),
+        lax.psum_scatter(grad_up.astype(jnp.bfloat16), ("regions", "shard"), scatter_dimension=0, tiled=True).astype(jnp.float32),
+        lax.psum_scatter(grad_down.astype(jnp.bfloat16), ("regions", "shard"), scatter_dimension=0, tiled=True).astype(jnp.float32),
         lax.psum_scatter(grad_vec, ("regions", "shard"), scatter_dimension=1, tiled=True),
     )
     mats_total = jnp.sum(mats_pages, axis=0)
@@ -315,7 +296,7 @@
         relative, grad_relative, first_relative, second_relative, 0.0
     )
     return (
-        result.astype(jnp.bfloat16)[None],
+        layer_out.astype(jnp.bfloat16)[None],
         in_grad[None],
         grad_qkv,
         firsts_qkv,

time: 973 us -> 815 us (0.84)
  waiting for transfers between devices: 181 us -> 408 us
  local copies, waits for them, and re-layouts: 164 us -> 23 us
  blocking collectives: 255 us -> 115 us
  other arithmetic: 141 us -> 34.8 us
  matrix products: 155 us -> 178 us
  starting transfers between devices: 52.7 us -> 30.8 us
    reduce_scatter x3 -> x4, waiting for transfers between devices: 0.01 us -> 285 us  [the longest x1 110 us: per_device(): lax.psum_scatter(grad_down.astype(jnp.bfloat16), ('regions', 'shard'), sc...]
    all_to_all x1 -> x0, blocking collectives: 172 us -> none  [per_device(): lax.all_to_all(pack_rows(grad_dense, home_rows, groups, slot_cap), 'regio...]
    scatter-add x1 -> x0, other arithmetic: 101 us -> none  [bias_table(): picked = relative[:, np.maximum(indices, 0)]]
    gather x8 -> x0, local copies, waits for them, and re-layouts: 92.1 us -> none  [the longest x2 59.9 us: bias_table(): picked = relative[:, np.maximum(indices, 0)]]
    all_to_all x3 -> x4, waiting for transfers between devices: 104 us -> 23.1 us  [exchange(): lax.all_to_all(packed.reshape(groups, slot_cap, rows.shape[1]), 'regions'...]
    unnamed x9 -> x8, waiting for transfers between devices: 58.6 us -> 2.65 us
    all_gather x1, waiting for transfers between devices: 0.02 us -> 54.5 us  [per_device(): lax.all_gather(w_up, ('regions', 'shard'), axis=0, tiled=True)]
    all_gather x1, waiting for transfers between devices: 0.01 us -> 43 us  [per_device(): lax.all_gather(w_down, ('regions', 'shard'), axis=0, tiled=True)]
  transfers between devices with their start and end apart: 11 -> 12, of which waited for: 5 -> 6; matrix products, arithmetic and copies ran while one was open for 44% -> 22% of each run, Pallas kernels for 0% -> 0%
where the time goes in v1:
time: 815 us; the launch traced here: 806 us
  waiting for transfers between devices  408 us (50%)
  matrix products  178 us (22%)
  blocking collectives  115 us (14%)
  other arithmetic  34.8 us (4%)
  starting transfers between devices  30.8 us (4%)
  local copies, waits for them, and re-layouts  23 us (3%)
  between operations  15.3 us (2%)
    reduce_scatter x1, waiting for transfers between devices, per_device(): lax.psum_scatter(grad_down.astype(jnp.bfloat16), ('regions', 'shard'), sc...  110 us
    reduce_scatter x1, waiting for transfers between devices, per_device(): lax.psum_scatter(grad_up.astype(jnp.bfloat16), ('regions', 'shard'), scat...  110 us
    all_gather x1, blocking collectives, per_device(): lax.all_gather(vectors, ('regions', 'shard'), axis=1, tiled=True)  69.1 us
    reduce_scatter x1, waiting for transfers between devices, per_device(): lax.psum_scatter(grad_qkv.astype(jnp.bfloat16), ('regions', 'shard'), sca...  64.8 us
    all_gather x1, waiting for transfers between devices, per_device(): lax.all_gather(w_up, ('regions', 'shard'), axis=0, tiled=True)  54.5 us
    unnamed x1, blocking collectives  46.1 us
    all_gather x1, waiting for transfers between devices, per_device(): lax.all_gather(w_down, ('regions', 'shard'), axis=0, tiled=True)  43 us
    all_to_all x4, starting transfers between devices, exchange(): lax.all_to_all(packed.reshape(groups, slot_cap, rows.shape[1]), 'regions'...  30 us
  transfers between devices with their start and end apart: 12, of which 6 were waited for; matrix products, arithmetic and copies ran while one was open for 22% of the time, Pallas kernels for 0%

profile of v1, /device:TPU:0, one launch (start us, length us, event | category | flops | bytes accessed | tf_op | source)
XLA Modules:
  0.0 805.5 jit_solution(9986579483285659051)
XLA Ops:
  10.2 2.8 convolution_convert_fusion.6
  13.0 8.5 %all-to-all-start = ((bf16[16,72,768]{2,1,0:T(8,128)(2,1)}), bf16[16,72,768]{2,1,0:T(8,128)(2,1)S(1)}, u32[]{:S(2)}, u32[]{:S(2)}) async-start(bf16[16,72,768]{2,1,0:T(8,128)(2,1)} %bitcast.132), calls=%async_computation | async-start | bytes 3538944 | tf_op jit(solution)/shard_map/all_to_all | solution.py:116
  22.2 69.1 %all-gather = bf16[32,24,12]{1,2,0:T(8,128)(2,1)S(1)} all-gather(bf16[1,24,12]{1,2,0:T(8,128)(2,1)S(1)} %bitcast.143), channel_id=1, replica_groups=mesh['regions'=16,'shard'=2] {'regions','shard'}, dimensions={0}, use_global_device_ids=true | all-gather | bytes 19008 | tf_op jit(solution)/shard_map/all_gather | solution.py:192
  95.4 4.0 convolution_convert_fusion.4
  99.4 1.8 fusion.42
  101.2 11.0 %fusion.12 = f32[12,576,576]{1,2,0:T(8,128)} fusion(f32[12,128,576]{1,2,0:T(8,128)S(1)} %fusion.42, s32[576]{0:T(1024)S(1)} %get-tuple-element.136, s32[576]{0:T(1024)S(1)} %get-tuple-element.137, s32[576]{0:T(1024)S(1)} %add_select_fusion), kind=kOutput, calls=%fused_computation.35 | convolution fusion | flops 6115663872 | bytes 19471104 | tf_op jit(solution)/shard_map/while/body/eval_jaxpr/hpb,qb->hpq/dot_general | solution.py:55
  112.3 7.4 all-to-all-start.2
  119.8 2.3 fusion.29
  122.1 4.5 add_convert_fusion.1
  126.6 2.9 copy.76
  129.5 15.4 %fusion.88 = (f32[12,576]{1,0:T(8,128)S(1)}, f32[12,576,576]{1,2,0:T(8,128)}) fusion(f32[12,576,576]{1,2,0:T(8,128)} %fusion.12, bf16[576,3,12,64]{0,3,2,1:T(8,128)(2,1)} %bitcast.117), kind=kOutput, calls=%fused_computation.179 | convolution fusion | flops 521544960 | bytes 35613696 | tf_op jit(solution)/shard_map/while/body/eval_jaxpr/phd,qhd->hpq/dot_general | solution.py:63
  144.9 8.6 %fusion = f32[12,576]{1,0:T(8,128)S(1)} fusion(f32[12,576,576]{1,2,0:T(8,128)} %get-tuple-element.124, f32[12,576]{1,0:T(8,128)S(1)} %get-tuple-element.123), kind=kLoop, calls=%fused_computation.6 | loop fusion | flops 7955712 | bytes 15980544 | tf_op jit(solution)/shard_map/while/body/eval_jaxpr/reduce_sum | solution.py:73
  153.5 10.6 %fusion.27 = bf16[12,64,576]{2,1,0:T(8,128)(2,1)} fusion(f32[12,576,576]{1,2,0:T(8,128)} %get-tuple-element.124, f32[12,576]{1,0:T(8,128)S(1)} %fusion, f32[12,576]{1,0:T(8,128)S(1)} %get-tuple-element.123, bf16[576,3,12,64]{0,3,2,1:T(8,128)(2,1)} %bitcast.118), kind=kOutput, calls=%fused_computation.78 | convolution fusion | flops 521994240 | bytes 19617792 | tf_op jit(solution)/shard_map/while/body/eval_jaxpr/hpq,qhd->phd/dot_general | solution.py:75
  164.1 2.9 fusion.89
  167.3 54.5 %all-gather.10.cloned.1.call-done = bf16[768,3072]{1,0:T(8,128)(2,1)} async-done(((bf16[24,3072]{1,0:T(8,128)(2,1)}), bf16[768,3072]{1,0:T(8,128)(2,1)}) %all-gather.10.cloned.1.call-update) | async-done | bytes 4718608 | tf_op jit(solution)/shard_map/all_gather | solution.py:190
  221.8 22.2 %multiply_convert_fusion.1 = (bf16[576,3072]{1,0:T(8,128)(2,1)}, f32[576,3072]{1,0:T(8,128)}, f32[576,3072]{1,0:T(8,128)}) fusion(f32[3072]{0:T(1024)S(1)} %copy-done.36, bf16[768,3072]{1,0:T(8,128)(2,1)} %all-gather.10.cloned.1.call-done, f32[576,768]{1,0:T(8,128)S(1)} %get-tuple-element.126, f32[768]{0:T(1024)S(1)} %get-tuple-element.79, ...), kind=kOutput, calls=%fused_computation.15 | convolution fusion | flops 2836905984 | bytes 24205824 | tf_op jit(solution)/shard_map/dot_general | solution.py:213
  244.0 43.0 %all-gather.12.cloned.1.call-done = bf16[3072,768]{1,0:T(8,128)(2,1)} async-done(((bf16[96,768]{1,0:T(8,128)(2,1)}), bf16[3072,768]{1,0:T(8,128)(2,1)}) %all-gather.12.cloned.1.call-update) | async-done | bytes 4718608 | tf_op jit(solution)/shard_map/all_gather | solution.py:191
  287.0 6.5 fusion.90
  295.2 4.0 multiply_reduce_fusion.1
  299.8 9.3 %convert_reduce_fusion = (f32[3072]{0:T(1024)S(1)}, bf16[576,3072]{1,0:T(8,128)(2,1)S(1)}) fusion(f32[576,3072]{1,0:T(8,128)} %get-tuple-element.116, bf16[3072,768]{1,0:T(8,128)(2,1)S(1)} %bitcast.147, f32[576,768]{1,0:T(8,128)S(1)} %get-tuple-element.94, f32[576,3072]{1,0:T(8,128)} %get-tuple-element.127, f32[3072]{0:T(1024)S(1)} %copy-done.36), kind=kOutput, calls=%fused_computation.13 | convolution fusion | flops 2748429312 | bytes 24207360 | tf_op jit(solution)/shard_map/td,fd->tf/dot_general | solution.py:225
  309.2 3.5 multiply_reduce_fusion.2
  314.5 2.1 convolution_convert_fusion.7
  316.6 2.4 convolution_convert_fusion.8
  319.6 11.5 %multiply_reduce_fusion = (f32[12,576]{1,0:T(8,128)S(1)}, f32[12,576,576]{1,2,0:T(8,128)}) fusion(f32[12,576,576]{1,2,0:T(8,128)} %get-tuple-element.124, f32[12,576]{1,0:T(8,128)S(1)} %log_add_fusion, bf16[576,12,64]{0,2,1:T(8,128)(2,1)S(1)} %bitcast.122, bf16[576,3,12,64]{0,3,2,1:T(8,128)(2,1)} %bitcast.119), kind=kOutput, calls=%fused_computation.1 | convolution fusion | flops 521544960 | bytes 35543040 | tf_op jit(solution)/shard_map/while/body/eval_jaxpr/phd,qhd->hpq/dot_general | solution.py:86
  331.1 12.6 %multiply_convert_fusion = bf16[12,576,576]{1,2,0:T(8,128)(2,1)S(1)} fusion(f32[12,576,576]{1,2,0:T(8,128)} %get-tuple-element.133, f32[12,576,576]{1,2,0:T(8,128)} %get-tuple-element.124, f32[12,576]{1,0:T(8,128)S(1)} %get-tuple-element.132, f32[12,576]{1,0:T(8,128)S(1)} %log_add_fusion), kind=kLoop, calls=%fused_computation | loop fusion | flops 15925248 | bytes 39868416 | tf_op jit(solution)/shard_map/while/body/eval_jaxpr/convert_element_type | solution.py:90
  343.7 2.7 multiply_bitcast_fusion
  347.2 2.7 multiply_bitcast_fusion.1
  349.9 8.9 %fusion.18 = bf16[576,1,12,64]{0,3,2,1:T(8,128)(2,1)S(1)} fusion(bf16[576,12,64]{0,2,1:T(8,128)(2,1)S(1)} %bitcast.123, f32[12,576,576]{1,2,0:T(8,128)} %get-tuple-element.124, f32[12,576]{1,0:T(8,128)S(1)} %log_add_fusion), kind=kOutput, calls=%fused_computation.68 | convolution fusion | flops 517570560 | bytes 17722368 | tf_op jit(solution)/shard_map/while/body/eval_jaxpr/hpq,phd->qhd/dot_general | solution.py:85
  361.1 4.5 convolution_convert_fusion
  367.1 7.8 convolution_convert_fusion.2
  376.4 3.1 convolution_convert_fusion.5
  379.5 4.4 all-to-all-start.1
  384.3 8.7 %convolution_convert_fusion.1 = bf16[3072,768]{1,0:T(8,128)(2,1)} fusion(bf16[576,3072]{1,0:T(8,128)(2,1)} %get-tuple-element.115, f32[576,768]{1,0:T(8,128)} %copy-done.11), kind=kOutput, calls=%fused_computation.33 | convolution fusion | flops 2720710656 | bytes 10027008 | tf_op jit(solution)/shard_map/tf,td->fd/dot_general | solution.py:224
  393.0 8.5 %convolution_convert_fusion.3 = bf16[1152,768]{1,0:T(8,128)(2,1)} fusion(s32[576]{0:T(1024)S(1)} %reduce.2, f32[576,768]{1,0:T(8,128)} %copy-done.12, bf16[576,2304]{0,1:T(8,128)(2,1)} %bitcast.125, bf16[768,2304]{1,0:T(8,128)(2,1)} %all-gather.6.cloned.1.call-done), kind=kOutput, calls=%fused_computation.37 | convolution fusion | flops 3060080640 | bytes 9734400 | tf_op jit(solution)/shard_map/dot_general | solution.py:115
  401.5 23.1 %all-to-all-done.1 = bf16[16,72,768]{2,1,0:T(8,128)(2,1)S(1)} async-done(((bf16[16,72,768]{2,1,0:T(8,128)(2,1)}), bf16[16,72,768]{2,1,0:T(8,128)(2,1)S(1)}, u32[]{:S(2)}, u32[]{:S(2)}) %all-to-all-start.1) | async-done | bytes 1769504 | tf_op jit(solution)/shard_map/all_to_all | solution.py:116
  424.6 9.8 %all-to-all-start.3 = ((bf16[16,72,768]{2,1,0:T(8,128)(2,1)}), bf16[16,72,768]{2,1,0:T(8,128)(2,1)}, u32[]{:S(2)}, u32[]{:S(2)}) async-start(bf16[16,72,768]{2,1,0:T(8,128)(2,1)} %bitcast.130), calls=%async_computation.3 | async-start | bytes 3538944 | tf_op jit(solution)/shard_map/all_to_all | solution.py:116
  438.6 6.6 fusion.57
  445.2 1.8 convolution_bitcast_fusion
  450.7 46.1 %all-reduce.15 = (f32[12,768]{1,0:T(8,128)S(1)}, f32[12,253]{1,0:T(8,128)S(1)}) all-reduce(f32[12,768]{1,0:T(8,128)S(1)} %concatenate.7, f32[12,253]{1,0:T(8,128)S(1)} %pad_add_fusion), channel_id=6, replica_groups=mesh['regions'=16,'shard'=2] {'regions','shard'}, use_global_device_ids=true, to_apply=%region_23.24.clone | all-reduce | flops 12252 | bytes 98016
  499.5 1.6 add_multiply_fusion.3
  501.2 2.3 fusion.34
  503.5 4.3 fusion.22
  507.8 64.8 %reduce-scatter.6.cloned.1.call-done = bf16[24,2304]{1,0:T(8,128)(2,1)} async-done(((bf16[768,2304]{1,0:T(8,128)(2,1)}), bf16[24,2304]{1,0:T(8,128)(2,1)}) %reduce-scatter.6.cloned.1.call-update) | async-done | bytes 110608 | tf_op jit(solution)/shard_map/reduce_scatter | solution.py:271
  572.6 1.8 add_multiply_fusion.2
  574.4 109.6 %reduce-scatter.10.cloned.1.call-done = bf16[24,3072]{1,0:T(8,128)(2,1)} async-done(((bf16[768,3072]{1,0:T(8,128)(2,1)}), bf16[24,3072]{1,0:T(8,128)(2,1)}) %reduce-scatter.10.cloned.1.call-update) | async-done | bytes 147472 | tf_op jit(solution)/shard_map/reduce_scatter | solution.py:273
  684.0 2.0 add_multiply_fusion.1
  686.0 110.5 %reduce-scatter.12.cloned.1.call-done = bf16[96,768]{1,0:T(8,128)(2,1)} async-done(((bf16[3072,768]{1,0:T(8,128)(2,1)}), bf16[96,768]{1,0:T(8,128)(2,1)}) %reduce-scatter.12.cloned.1.call-update) | async-done | bytes 147472 | tf_op jit(solution)/shard_map/reduce_scatter | solution.py:274
  796.5 2.0 add_multiply_fusion
  (203 shorter events, 29.7 us)
Async XLA Ops:
  7.2 114.8 %all-gather.6.cloned.1.call-start = ((), (), s32[]{:S(2)}) async-start(), calls=%async_computation.8 | async-start | bytes 3649536 | tf_op jit(solution)/shard_map/all_gather | solution.py:188
  8.0 156.1 %all-gather.8.cloned.1.call-start = ((), (), s32[]{:S(2)}) async-start(), calls=%async_computation.9 | async-start | bytes 1216512 | tf_op jit(solution)/shard_map/all_gather | solution.py:189
  8.7 213.1 %all-gather.10.cloned.1.call-start = ((), (), s32[]{:S(2)}) async-start(), calls=%async_computation.10 | async-start | bytes 4866048 | tf_op jit(solution)/shard_map/all_gather | solution.py:190
  10.1 85.2 %copy-start.38 = (s32[576]{0:T(1024)}, s32[576]{0:T(1024)S(1)}, u32[]{:S(2)}) copy-start(s32[576]{0:T(1024)S(1)} %reduce.1) | copy-start | bytes 6916
  13.0 9.1 %copy-start.40 = (s32[1,576]{1,0:T(1,128)S(1)}, s32[1,576]{1,0:T(1,128)}, u32[]{:S(2)}) copy-start(s32[1,576]{1,0:T(1,128)} %param.45) | copy-start | bytes 6916
  13.0 9.1 %copy-start.24 = (f32[12,253]{1,0:T(8,128)S(1)}, f32[12,253]{1,0:T(8,128)}, u32[]{:S(2)}) copy-start(f32[12,253]{1,0:T(8,128)} %param.31) | copy-start | bytes 36436
  13.0 9.2 %copy-start.34 = (bf16[12,24]{1,0:T(8,128)(2,1)S(1)}, bf16[12,24]{1,0:T(8,128)(2,1)}, u32[]{:S(2)}) copy-start(bf16[12,24]{1,0:T(8,128)(2,1)} %param.30) | copy-start | bytes 1732
  13.0 80.4 %copy-start.43 = (pred[128]{0:T(512)(128)(4,1)S(1)}, pred[128]{0:T(512)(128)(4,1)}, u32[]{:S(2)}) copy-start(pred[128]{0:T(512)(128)(4,1)} %constant.53.clone.1) | copy-start | bytes 388
  13.0 99.3 %all-to-all-start = ((bf16[16,72,768]{2,1,0:T(8,128)(2,1)}), bf16[16,72,768]{2,1,0:T(8,128)(2,1)S(1)}, u32[]{:S(2)}, u32[]{:S(2)}) async-start(bf16[16,72,768]{2,1,0:T(8,128)(2,1)} %bitcast.132), calls=%async_computation | async-start | bytes 3538944 | tf_op jit(solution)/shard_map/all_to_all | solution.py:116
  21.4 265.6 %all-gather.12.cloned.1.call-start = ((), (), s32[]{:S(2)}) async-start(), calls=%async_computation.11 | async-start | bytes 4866048 | tf_op jit(solution)/shard_map/all_gather | solution.py:191
  94.7 6.5 copy-start.26
  95.4 5.9 copy-start.28
  95.4 5.9 copy-start.30
  112.3 182.8 %all-to-all-start.2 = ((bf16[16,72,768]{2,1,0:T(8,128)(2,1)}), bf16[16,72,768]{2,1,0:T(8,128)(2,1)}, u32[]{:S(2)}, u32[]{:S(2)}) async-start(bf16[16,72,768]{2,1,0:T(8,128)(2,1)} %bitcast.133), calls=%async_computation.2 | async-start | bytes 3538944 | tf_op jit(solution)/shard_map/all_to_all | solution.py:116
  119.7 379.8 %reduce-scatter.8.cloned.1.call-start = ((), (), s32[]{:S(2)}) async-start(), calls=%async_computation.13 | async-start | bytes 1216512 | tf_op jit(solution)/shard_map/reduce_scatter | solution.py:272
  164.1 57.7 %copy-start.36 = (f32[3072]{0:T(1024)S(1)}, f32[3072]{0:T(1024)}, u32[]{:S(2)}) copy-start(f32[3072]{0:T(1024)} %add.291) | copy-start | bytes 36868
  166.9 145.7 %copy-start.4 = (f32[576,768]{1,0:T(8,128)}, f32[576,768]{1,0:T(8,128)S(1)}, u32[]{:S(2)}) copy-start(f32[576,768]{1,0:T(8,128)S(1)} %get-tuple-element.126) | copy-start | bytes 5308420
  295.1 4.6 slice-start.2
  295.1 4.6 slice-start.3
  299.2 10.0 %slice-start = ((s8[4718592]{0:T(1024)(128)(4,1)}), s8[524288]{0:T(1024)(128)(4,1)S(1)}, s32[]{:S(2)}) async-start(s8[4718592]{0:T(1024)(128)(4,1)} %bitcast.144), calls=%async_computation.16 | async-start | bytes 1048576
  299.7 9.4 %copy-start.11 = (f32[576,768]{1,0:T(8,128)}, f32[576,768]{1,0:T(8,128)S(1)}, u32[]{:S(2)}) copy-start(f32[576,768]{1,0:T(8,128)S(1)} %get-tuple-element.94) | copy-start | bytes 5308420
  299.8 9.4 %slice-start.1 = ((s8[4718592]{0:T(1024)(128)(4,1)}), s8[4194304]{0:T(1024)(128)(4,1)S(1)}, s32[]{:S(2)}) async-start(s8[4718592]{0:T(1024)(128)(4,1)} %bitcast.144), calls=%async_computation.17 | async-start | bytes 8388608
  331.1 12.6 %copy-start.3 = (bf16[576,2304]{0,1:T(8,128)(2,1)S(1)}, bf16[576,2304]{0,1:T(8,128)(2,1)}, u32[]{:S(2)}) copy-start(bf16[576,2304]{0,1:T(8,128)(2,1)} %copy.76) | copy-start | bytes 7962628
  349.9 222.7 %reduce-scatter.6.cloned.1.call-start = ((), (), s32[]{:S(2)}) async-start(), calls=%async_computation.12 | async-start | bytes 3649536 | tf_op jit(solution)/shard_map/reduce_scatter | solution.py:271
  349.9 8.9 %copy-start.9 = (bf16[576,1,12,64]{0,3,2,1:T(8,128)(2,1)S(1)}, bf16[576,1,12,64]{0,3,2,1:T(8,128)(2,1)}, u32[]{:S(2)}) copy-start(bf16[576,1,12,64]{0,3,2,1:T(8,128)(2,1)} %multiply_bitcast_fusion.1) | copy-start | bytes 2654212
  365.6 318.4 %reduce-scatter.10.cloned.1.call-start = ((), (), s32[]{:S(2)}) async-start(), calls=%async_computation.14 | async-start | bytes 4866048 | tf_op jit(solution)/shard_map/reduce_scatter | solution.py:273
  379.5 45.1 %all-to-all-start.1 = ((bf16[16,72,768]{2,1,0:T(8,128)(2,1)}), bf16[16,72,768]{2,1,0:T(8,128)(2,1)S(1)}, u32[]{:S(2)}, u32[]{:S(2)}) async-start(bf16[16,72,768]{2,1,0:T(8,128)(2,1)} %bitcast.134), calls=%async_computation.1 | async-start | bytes 3538944 | tf_op jit(solution)/shard_map/all_to_all | solution.py:116
  383.9 412.6 %reduce-scatter.12.cloned.1.call-start = ((), (), s32[]{:S(2)}) async-start(), calls=%async_computation.15 | async-start | bytes 4866048 | tf_op jit(solution)/shard_map/reduce_scatter | solution.py:274
  401.5 37.1 %copy-start.27 = (s32[576]{0:T(1024)S(1)}, s32[576]{0:T(1024)}, u32[]{:S(2)}) copy-start(s32[576]{0:T(1024)} %copy-done.26) | copy-start | bytes 6916
  401.5 37.1 %copy-start.29 = (s32[576]{0:T(1024)S(1)}, s32[576]{0:T(1024)}, u32[]{:S(2)}) copy-start(s32[576]{0:T(1024)} %copy-done.28) | copy-start | bytes 6916
  401.5 37.1 %copy-start.31 = (s32[576]{0:T(1024)S(1)}, s32[576]{0:T(1024)}, u32[]{:S(2)}) copy-start(s32[576]{0:T(1024)} %copy-done.30) | copy-start | bytes 6916
  424.6 78.9 %all-to-all-start.3 = ((bf16[16,72,768]{2,1,0:T(8,128)(2,1)}), bf16[16,72,768]{2,1,0:T(8,128)(2,1)}, u32[]{:S(2)}, u32[]{:S(2)}) async-start(bf16[16,72,768]{2,1,0:T(8,128)(2,1)} %bitcast.130), calls=%async_computation.3 | async-start | bytes 3538944 | tf_op jit(solution)/shard_map/all_to_all | solution.py:116
  447.9 48.8 %copy-start.35 = (bf16[12,24]{1,0:T(8,128)(2,1)S(1)}, bf16[12,24]{1,0:T(8,128)(2,1)}, u32[]{:S(2)}) copy-start(bf16[12,24]{1,0:T(8,128)(2,1)} %param.30) | copy-start | bytes 1732
  448.0 50.2 %copy-start.25 = (f32[12,253]{1,0:T(8,128)S(1)}, f32[12,253]{1,0:T(8,128)}, u32[]{:S(2)}) copy-start(f32[12,253]{1,0:T(8,128)} %param.31) | copy-start | bytes 36436
  448.0 51.6 %copy-start.23 = (bf16[24,768]{1,0:T(8,128)(2,1)S(1)}, bf16[24,768]{1,0:T(8,128)(2,1)}, u32[]{:S(2)}) copy-start(bf16[24,768]{1,0:T(8,128)(2,1)} %param.27) | copy-start | bytes 110596
  448.0 51.6 %copy-start.32 = (f32[24,768]{1,0:T(8,128)S(1)}, f32[24,768]{1,0:T(8,128)}, u32[]{:S(2)}) copy-start(f32[24,768]{1,0:T(8,128)} %param.35) | copy-start | bytes 221188
  448.3 52.8 %copy-start.39 = (s32[576]{0:T(1024)S(1)}, s32[576]{0:T(1024)}, u32[]{:S(2)}) copy-start(s32[576]{0:T(1024)} %copy-done.38) | copy-start | bytes 6916
  496.7 6.7 copy-start.33
  503.5 69.1 %copy-start.16 = (bf16[24,2304]{1,0:T(8,128)(2,1)S(1)}, bf16[24,2304]{1,0:T(8,128)(2,1)}, u32[]{:S(2)}) copy-start(bf16[24,2304]{1,0:T(8,128)(2,1)} %param.26) | copy-start | bytes 331780
  503.5 69.1 %copy-start.21 = (f32[24,2304]{1,0:T(8,128)S(1)}, f32[24,2304]{1,0:T(8,128)}, u32[]{:S(2)}) copy-start(f32[24,2304]{1,0:T(8,128)} %param.33) | copy-start | bytes 663556
  503.5 69.1 %copy-start.22 = (f32[24,2304]{1,0:T(8,128)S(1)}, f32[24,2304]{1,0:T(8,128)}, u32[]{:S(2)}) copy-start(f32[24,2304]{1,0:T(8,128)} %param.32) | copy-start | bytes 663556
  503.5 180.5 %copy-start.14 = (bf16[24,3072]{1,0:T(8,128)(2,1)S(1)}, bf16[24,3072]{1,0:T(8,128)(2,1)}, u32[]{:S(2)}) copy-start(bf16[24,3072]{1,0:T(8,128)(2,1)} %param.28) | copy-start | bytes 442372
  503.5 180.5 %copy-start.17 = (f32[24,3072]{1,0:T(8,128)S(1)}, f32[24,3072]{1,0:T(8,128)}, u32[]{:S(2)}) copy-start(f32[24,3072]{1,0:T(8,128)} %param.37) | copy-start | bytes 884740
  503.5 180.5 %copy-start.18 = (f32[24,3072]{1,0:T(8,128)S(1)}, f32[24,3072]{1,0:T(8,128)}, u32[]{:S(2)}) copy-start(f32[24,3072]{1,0:T(8,128)} %param.36) | copy-start | bytes 884740
  503.5 295.0 %copy-start.1 = (bf16[1,576,768]{2,1,0:T(8,128)(2,1)S(1)}, bf16[1,576,768]{2,1,0:T(8,128)(2,1)}, u32[]{:S(2)}) copy-start(bf16[1,576,768]{2,1,0:T(8,128)(2,1)} %param.24) | copy-start | bytes 2654212
  507.8 288.7 %copy-start.15 = (bf16[96,768]{1,0:T(8,128)(2,1)S(1)}, bf16[96,768]{1,0:T(8,128)(2,1)}, u32[]{:S(2)}) copy-start(bf16[96,768]{1,0:T(8,128)(2,1)} %param.29) | copy-start | bytes 442372
  507.8 288.7 %copy-start.19 = (f32[96,768]{1,0:T(8,128)S(1)}, f32[96,768]{1,0:T(8,128)}, u32[]{:S(2)}) copy-start(f32[96,768]{1,0:T(8,128)} %param.39) | copy-start | bytes 884740
  507.8 288.7 %copy-start.20 = (f32[96,768]{1,0:T(8,128)S(1)}, f32[96,768]{1,0:T(8,128)}, u32[]{:S(2)}) copy-start(f32[96,768]{1,0:T(8,128)} %param.38) | copy-start | bytes 884740
  (16 other events, 38.3 us)
Sparse Core Ops, SparseCore 0:
  11.0 75.6 all-gather.5
  89.5 63.0 all-gather.7
  155.6 66.1 all-gather.9
  224.6 62.4 all-gather.11
  350.0 112.7 reduce-scatter.7
  468.1 104.4 reduce-scatter.5
  578.0 105.9 reduce-scatter.9
  690.4 106.0 reduce-scatter.11

commit v2 on v1

--- a/solution.py
+++ b/solution.py
@@ -1,7 +1,10 @@
+import functools
 import jax
 import jax.numpy as jnp
 import numpy as np
 from jax import lax
+from jax.experimental import pallas as pl
+from jax.experimental.pallas import tpu as pltpu
 from jax.sharding import PartitionSpec as P
 
 HEADS = 12
@@ -150,7 +153,563 @@
     return (moment_new, square_new, update)
 
 
+MESH = pl.DeviceIdType.MESH
+PEERS = 16
+VEC_COLS = 256
+
+
+def place():
+    me = lax.axis_index("regions")
+    core = lax.axis_index("shard")
+    z = lax.div(me, 4)
+    y = lax.div(lax.rem(me, 4), 2)
+    x = lax.rem(me, 2)
+    return me, core, z, y, x
+
+
+def enter(me, core):
+    barrier = pltpu.get_barrier_semaphore()
+    for k in range(1, PEERS):
+        pl.semaphore_signal(barrier, inc=1, device_id=(me ^ k, core), device_id_type=MESH)
+    pl.semaphore_signal(barrier, inc=1, device_id=(me, 1 - core), device_id_type=MESH)
+    pl.semaphore_wait(barrier, PEERS)
+
+
+def remote(src, dst, send, recv, device):
+    return pltpu.make_async_remote_copy(
+        src_ref=src, dst_ref=dst, send_sem=send, recv_sem=recv, device_id=device, device_id_type=MESH
+    )
+
+
+class Exchange:
+    def __init__(self, where, packed, arrived, send, recv, local):
+        self.me, self.core = where[0], where[1]
+        self.packed, self.arrived = packed, arrived
+        self.send, self.recv, self.local = send, recv, local
+        self.slots, self.half = packed.shape[1], packed.shape[2]
+
+    def pack(self, rows, row_of):
+        left, right = rows[:, : self.half], rows[:, self.half :]
+
+        def one(k, carry):
+            d = self.me ^ k
+            base = d * self.slots
+            at = lax.broadcasted_iota(jnp.int32, (self.slots, rows.shape[0]), 0) + base
+            target = row_of[...]
+            lefts = jnp.where(at == target, 1.0, 0.0).astype(jnp.bfloat16)
+            rights = jnp.where(at == target + self.slots // 2, 1.0, 0.0).astype(jnp.bfloat16)
+            block = jnp.dot(lefts, left, preferred_element_type=jnp.float32) + jnp.dot(
+                rights, right, preferred_element_type=jnp.float32
+            )
+            self.packed[d] = block.astype(jnp.bfloat16)
+
+            @pl.when(k > 0)
+            def _():
+                self.copy(k).start()
+
+            return carry
+
+        lax.fori_loop(0, PEERS, one, 0)
+        self.own().start()
+
+    def copy(self, k):
+        d = self.me ^ k
+        return remote(
+            self.packed.at[d], self.arrived.at[self.me], self.send.at[k], self.recv.at[k], (d, self.core)
+        )
+
+    def own(self):
+        return pltpu.make_async_copy(self.packed.at[self.me], self.arrived.at[self.me], self.local)
+
+    def wait(self):
+        self.own().wait()
+
+        def one(k, carry):
+            self.copy(k).wait()
+            return carry
+
+        lax.fori_loop(1, PEERS, one, 0)
+
+    def unpack(self, row_of, out, kind):
+        total = PEERS * self.slots
+        for part in range(2):
+            wanted = row_of[...] + part * (self.slots // 2)
+            at = lax.broadcasted_iota(jnp.int32, (out.shape[0], total), 1)
+            picking = jnp.where(at == wanted, 1.0, 0.0).astype(jnp.bfloat16)
+            got = jnp.dot(
+                picking,
+                self.arrived[...].reshape(total, self.half),
+                preferred_element_type=jnp.float32,
+            )
+            out[:, part * self.half : (part + 1) * self.half] = got.astype(kind)
+
+
+def pieces_of(rows, half):
+    if rows % 32 == 0:
+        return [(0, rows // 2, 0, half, True), (rows // 2, rows // 2, 0, half, False)]
+    cut = (half // 128 + 1) // 2 * 128
+    return [(0, rows, 0, cut, True), (0, rows, cut, half - cut, False)]
+
+
+class Gather:
+    STAGES = 7
+
+    def __init__(self, where, whole, piece, sems):
+        self.where, self.whole, self.piece, self.sems = where, whole, piece, sems
+
+    def part(self, z, y, x):
+        core = self.where[1]
+        r0, rows, c0, cols, _ = self.piece
+        half = self.whole.shape[4] // 2
+        at = pl.multiple_of(core * half + c0, 128)
+        return self.whole.at[z, y, x, pl.ds(r0, rows), pl.ds(at, cols)]
+
+    def along_z(self, t, upward):
+        me, core, z, y, x = self.where
+        step = 1 if upward else -1
+        origin = z - step * t
+        ref = self.part(origin, y, x)
+        i = 2 * t + (1 if upward else 0)
+        return remote(ref, ref, self.sems.at[0, i], self.sems.at[1, i], (me + 4 * step, core))
+
+    def z_sends(self, t, do):
+        z = self.where[2]
+
+        @pl.when((z >= t) & (z <= 2))
+        def _():
+            do(self.along_z(t, True))
+
+        @pl.when((z + t <= 3) & (z >= 1))
+        def _():
+            do(self.along_z(t, False))
+
+    def z_waits(self, t):
+        z = self.where[2]
+
+        @pl.when(z - 1 - t >= 0)
+        def _():
+            me, core, z, y, x = self.where
+            ref = self.part(z - 1 - t, y, x)
+            i = 2 * t + 1
+            remote(ref, ref, self.sems.at[0, i], self.sems.at[1, i], (me, 1 - core)).wait_recv()
+
+        @pl.when(z + 1 + t <= 3)
+        def _():
+            me, core, z, y, x = self.where
+            ref = self.part(z + 1 + t, y, x)
+            i = 2 * t
+            remote(ref, ref, self.sems.at[0, i], self.sems.at[1, i], (me, 1 - core)).wait_recv()
+
+    def plane(self, n):
+        me, core, z, y, x = self.where
+        x_first = self.piece[4]
+        every = slice(None)
+        if n == 2:
+            ref, device = self.part(every, every, every), (me, 1 - core)
+        elif n == 0:
+            ref, device = self.part(every, y, x), (me ^ (1 if x_first else 2), core)
+        elif x_first:
+            ref, device = self.part(every, y, every), (me ^ 2, core)
+        else:
+            ref, device = self.part(every, every, x), (me ^ 1, core)
+        return remote(ref, ref, self.sems.at[0, 6 + n], self.sems.at[1, 6 + n], device)
+
+    def run(self, stage):
+        if stage < 3:
+            if stage:
+                self.z_waits(stage - 1)
+            self.z_sends(stage, lambda copy: copy.start())
+        elif stage == 3:
+            self.z_waits(2)
+            self.plane(0).start()
+        elif stage < 6:
+            self.plane(stage - 4).wait_recv()
+            self.plane(stage - 3).start()
+        else:
+            self.plane(2).wait_recv()
+
+    def sent(self):
+        for t in range(3):
+            self.z_sends(t, lambda copy: copy.wait_send())
+        for n in range(3):
+            self.plane(n).wait_send()
+
+
+class Scatter:
+    STAGES = 9
+
+    def __init__(self, where, local, sums, from_core, from_near, from_far, from_z, piece, sems):
+        self.where, self.local, self.sums, self.piece, self.sems = where, local, sums, piece, sems
+        self.from_core, self.from_near, self.from_far, self.from_z = from_core, from_near, from_far, from_z
+        self.half = sums.shape[4]
+
+    def cut(self, ref, *lead, core=None):
+        r0, rows, c0, cols, _ = self.piece
+        at = c0 if core is None else pl.multiple_of(core * self.half + c0, 128)
+        return ref.at[(*lead, pl.ds(r0, rows), pl.ds(at, cols))]
+
+    def between_cores(self):
+        me, core = self.where[0], self.where[1]
+        every = slice(None)
+        src = self.cut(self.local, every, every, every, core=1 - core)
+        dst = self.cut(self.from_core, every, every, every)
+        return remote(src, dst, self.sems.at[0, 0], self.sems.at[1, 0], (me, 1 - core))
+
+    def near(self):
+        me, core, z, y, x = self.where
+        every = slice(None)
+        if self.piece[4]:
+            src, device = self.cut(self.sums, every, 1 - y, every), (me ^ 2, core)
+        else:
+            src, device = self.cut(self.sums, every, every, 1 - x), (me ^ 1, core)
+        dst = self.cut(self.from_near, every, every)
+        return remote(src, dst, self.sems.at[0, 1], self.sems.at[1, 1], device)
+
+    def far(self):
+        me, core, z, y, x = self.where
+        every = slice(None)
+        if self.piece[4]:
+            src, device = self.cut(self.sums, every, y, 1 - x), (me ^ 1, core)
+        else:
+            src, device = self.cut(self.sums, every, 1 - y, x), (me ^ 2, core)
+        dst = self.cut(self.from_far, every)
+        return remote(src, dst, self.sems.at[0, 2], self.sems.at[1, 2], device)
+
+    def along_z(self, sender, upward):
+        me, core, z, y, x = self.where
+        lead = pl.ds(sender + 1, 3 - sender) if upward else pl.ds(0, sender)
+        src = self.cut(self.sums, lead, y, x)
+        dst = self.cut(self.from_z, 1 if upward else 0, lead)
+        i = 3 + (1 if upward else 0)
+        step = 4 if upward else -4
+        return remote(src, dst, self.sems.at[0, i], self.sems.at[1, i], (me + step, core))
+
+    def add(self, target, other):
+        total = target[...].astype(jnp.float32) + other[...].astype(jnp.float32)
+        target[...] = total.astype(jnp.bfloat16)
+
+    def z_got(self, sender, upward):
+        me, core, z, y, x = self.where
+        self.along_z(sender, upward).wait_recv()
+        for d in range(sender + 1, 4) if upward else range(sender):
+            self.add(self.cut(self.sums, d, y, x), self.cut(self.from_z, 1 if upward else 0, d))
+
+    def run(self, stage):
+        me, core, z, y, x = self.where
+        if stage == 0:
+            self.between_cores().start()
+        elif stage == 1:
+            self.between_cores().wait_recv()
+
+            def one(i, carry):
+                a, b, c = lax.div(i, 4), lax.div(lax.rem(i, 4), 2), lax.rem(i, 2)
+                mine = self.cut(self.local, a, b, c, core=core)[...].astype(jnp.float32)
+                other = self.cut(self.from_core, a, b, c)[...].astype(jnp.float32)
+                self.cut(self.sums, a, b, c)[...] = (mine + other).astype(jnp.bfloat16)
+                return carry
+
+            lax.fori_loop(0, 16, one, 0)
+            self.near().start()
+        elif stage == 2:
+            self.near().wait_recv()
+
+            def one(i, carry):
+                a, b = lax.div(i, 2), lax.rem(i, 2)
+                target = self.cut(self.sums, a, y, b) if self.piece[4] else self.cut(self.sums, a, b, x)
+                self.add(target, self.cut(self.from_near, a, b))
+                return carry
+
+            lax.fori_loop(0, 8, one, 0)
+            self.far().start()
+        elif stage == 3:
+            self.far().wait_recv()
+
+            def one(i, carry):
+                self.add(self.cut(self.sums, i, y, x), self.cut(self.from_far, i))
+                return carry
+
+            lax.fori_loop(0, 4, one, 0)
+
+            @pl.when(z == 3)
+            def _():
+                self.along_z(3, False).start()
+
+            @pl.when(z == 0)
+            def _():
+                self.along_z(0, True).start()
+
+        elif stage == 4:
+
+            @pl.when(z == 2)
+            def _():
+                self.z_got(3, False)
+                self.along_z(2, False).start()
+
+            @pl.when(z == 1)
+            def _():
+                self.z_got(0, True)
+                self.along_z(1, True).start()
+
+        elif stage == 5:
+
+            @pl.when(z == 1)
+            def _():
+                self.z_got(2, False)
+                self.along_z(1, False).start()
+
+            @pl.when(z == 2)
+            def _():
+                self.z_got(1, True)
+                self.along_z(2, True).start()
+
+        elif stage == 6:
+
+            @pl.when(z == 0)
+            def _():
+                self.z_got(1, False)
+
+            @pl.when(z == 3)
+            def _():
+                self.z_got(2, True)
+
+    def sent(self):
+        z = self.where[2]
+        self.between_cores().wait_send()
+        self.near().wait_send()
+        self.far().wait_send()
+        for sender in range(4):
+
+            @pl.when(z == sender)
+            def _(sender=sender):
+                if sender > 0:
+                    self.along_z(sender, False).wait_send()
+                if sender < 3:
+                    self.along_z(sender, True).wait_send()
+
+
+def staggered(tasks, stages, extra=None):
+    for k in range(len(tasks) + stages - 1):
+        for i, task in enumerate(tasks):
+            if 0 <= k - i < stages:
+                task.run(k - i)
+        if extra is not None:
+            extra(k)
+
+
+def inbound_kernel(
+    rows_ref, grad_ref, slot_line, home_column, s_qkv, s_out, s_up, s_down,
+    homed, cotangent, w_qkv, w_out, w_up, w_down,
+    packed_a, arrived_a, packed_b, arrived_b, p_qkv, p_out, p_up, p_down, b_qkv, b_out, b_up, b_down,
+    send_a, recv_a, send_b, recv_b, local_sems, pair_sems, block_sems, piece_sems,
+):
+    where = place()
+    me, core, z, y, x = where
+    enter(me, core)
+    shards = (s_qkv, s_out, s_up, s_down)
+    others = (p_qkv, p_out, p_up, p_down)
+    blocks = (b_qkv, b_out, b_up, b_down)
+    wholes = (w_qkv, w_out, w_up, w_down)
+    pairs = [
+        remote(shards[i].at[1 - core], others[i], pair_sems.at[0, i], pair_sems.at[1, i], (me, 1 - core))
+        for i in range(4)
+    ]
+    for pair in pairs:
+        pair.start()
+    moved = Exchange(where, packed_a, arrived_a, send_a, recv_a, local_sems.at[0])
+    moved_grad = Exchange(where, packed_b, arrived_b, send_b, recv_b, local_sems.at[1])
+    moved.pack(rows_ref, slot_line)
+    placed = []
+    tasks = []
+    for i in range(4):
+        pairs[i].wait_recv()
+        half = blocks[i].shape[1]
+        rows = blocks[i].shape[0] // 2
+        mine = shards[i][core][:rows].astype(jnp.float32)
+        other = others[i][:rows].astype(jnp.float32)
+        first = jnp.where(core == 0, mine, other)
+        second = jnp.where(core == 0, other, mine)
+        blocks[i][...] = jnp.concatenate([first, second], axis=0).astype(jnp.bfloat16)
+        at = pl.multiple_of(core * half, 128)
+        copy = pltpu.make_async_copy(
+            blocks[i], wholes[i].at[z, y, x, :, pl.ds(at, half)], block_sems.at[i]
+        )
+        copy.start()
+        placed.append(copy)
+    for i in range(4):
+        placed[i].wait()
+        for piece in pieces_of(blocks[i].shape[0], blocks[i].shape[1]):
+            n = len(tasks)
+            tasks.append(Gather(where, wholes[i], piece, piece_sems.at[n]))
+
+    def extra(k):
+        if k == 2:
+            moved_grad.pack(grad_ref, slot_line)
+
+    staggered(tasks, Gather.STAGES, extra)
+    moved.wait()
+    moved.unpack(home_column, homed, jnp.bfloat16)
+    moved_grad.wait()
+    moved_grad.unpack(home_column, cotangent, jnp.bfloat16)
+    for pair in pairs:
+        pair.wait_send()
+    for task in tasks:
+        task.sent()
+
+
+def vmem(count):
+    return [pl.BlockSpec(memory_space=pltpu.VMEM)] * count
+
+
+def inbound(rows, grads, slot_line, home_column, shards):
+    tokens, width = rows.shape
+    slots = 2 * (2 * tokens // PEERS)
+    buffer = pltpu.VMEM((PEERS, slots, width // 2), jnp.bfloat16)
+    wholes, pair_shapes, block_shapes = [], [], []
+    for shard, padded in shards:
+        half = padded.shape[2]
+        wholes.append(jax.ShapeDtypeStruct((4, 2, 2, 2 * shard, 2 * half), jnp.bfloat16))
+        pair_shapes.append(pltpu.VMEM(padded.shape[1:], jnp.bfloat16))
+        block_shapes.append(pltpu.VMEM((2 * shard, half), jnp.bfloat16))
+    dma = pltpu.SemaphoreType.DMA
+    return pl.pallas_call(
+        inbound_kernel,
+        out_shape=[jax.ShapeDtypeStruct(rows.shape, jnp.bfloat16)] * 2 + wholes,
+        in_specs=vmem(8),
+        out_specs=vmem(6),
+        scratch_shapes=[buffer] * 4 + pair_shapes + block_shapes
+        + [dma((PEERS,)), dma((PEERS,)), dma((PEERS,)), dma((PEERS,)), dma((2,)), dma((2, 4)), dma((4,)), dma((8, 2, 9))],
+        compiler_params=pltpu.CompilerParams(
+            collective_id=1, has_side_effects=True, vmem_limit_bytes=60 << 20
+        ),
+        name="inbound",
+    )(rows, grads, slot_line, home_column, *[padded for _, padded in shards])
+
+
+def outbound_kernel(
+    result_ref, grad_ref, home_line, slot_column, table_ref, g_qkv, g_out, g_up, g_down,
+    result_out, grad_out, table_out, o_qkv, o_out, o_up, o_down,
+    packed_a, arrived_a, packed_b, arrived_b, table_got,
+    t_qkv, t_out, t_up, t_down, c_qkv, c_out, c_up, c_down, n_qkv, n_out, n_up, n_down,
+    f_qkv, f_out, f_up, f_down, z_qkv, z_out, z_up, z_down, e_qkv, e_out, e_up, e_down,
+    send_a, recv_a, send_b, recv_b, local_sems, table_sems, piece_sems, last_sems,
+):
+    where = place()
+    me, core, z, y, x = where
+    enter(me, core)
+    local = (g_qkv, g_out, g_up, g_down)
+    sums = (t_qkv, t_out, t_up, t_down)
+    from_core = (c_qkv, c_out, c_up, c_down)
+    from_near = (n_qkv, n_out, n_up, n_down)
+    from_far = (f_qkv, f_out, f_up, f_down)
+    from_z = (z_qkv, z_out, z_up, z_down)
+    ends = (e_qkv, e_out, e_up, e_down)
+    outs = (o_qkv, o_out, o_up, o_down)
+    tasks = []
+    for i in (3, 2, 1, 0):
+        for piece in pieces_of(sums[i].shape[3], sums[i].shape[4]):
+            n = len(tasks)
+            tasks.append(
+                Scatter(where, local[i], sums[i], from_core[i], from_near[i], from_far[i], from_z[i], piece, piece_sems.at[n])
+            )
+    moved = Exchange(where, packed_a, arrived_a, send_a, recv_a, local_sems.at[0])
+    moved_grad = Exchange(where, packed_b, arrived_b, send_b, recv_b, local_sems.at[1])
+    table_out[...] = table_ref[...]
+    steps = [(me, 1 - core), (me ^ 1, core), (me ^ 2, core), (me ^ 4, core), (me ^ 8, core)]
+    shares = [
+        remote(table_got.at[0, n], table_got.at[1, n], table_sems.at[0, n], table_sems.at[1, n], device)
+        for n, device in enumerate(steps)
+    ]
+
+    def extra(k):
+        if k == 0:
+            moved.pack(result_ref, home_line)
+        if k == 3:
+            moved_grad.pack(grad_ref, home_line)
+        if 4 <= k <= 9:
+            n = k - 4
+            if n > 0:
+                shares[n - 1].wait_recv()
+                table_out[...] += table_got[1, n - 1]
+            if n < 5:
+                table_got[0, n] = table_out[...]
+                shares[n].start()
+
+    staggered(tasks, 7, extra)
+    finals = []
+    for i in (3, 2, 1, 0):
+        block = sums[i][z, y, x].astype(jnp.float32)
+        rows = block.shape[0] // 2
+        ends[i][0] = block[:rows]
+        ends[i][1] = block[rows:]
+        outs[i][core] = ends[i][core]
+        copy = remote(ends[i].at[1 - core], outs[i].at[core], last_sems.at[0, i], last_sems.at[1, i], (me, 1 - core))
+        copy.start()
+        finals.append(copy)
+    moved.wait()
+    moved.unpack(slot_column, result_out, jnp.bfloat16)
+    moved_grad.wait()
+    moved_grad.unpack(slot_column, grad_out, jnp.float32)
+    for copy in finals:
+        copy.wait()
+    for share in shares:
+        share.wait_send()
+    for task in tasks:
+        task.sent()
+
+
+def outbound(result, grads, home_line, slot_column, table, locals_):
+    tokens, width = result.shape
+    slots = 2 * (2 * tokens // PEERS)
+    buffer = pltpu.VMEM((PEERS, slots, width // 2), jnp.bfloat16)
+    halves = [(g.shape[3], g.shape[4] // 2) for g in locals_]
+    low = jnp.bfloat16
+    scratch = (
+        [buffer] * 4
+        + [pltpu.VMEM((2, 5, *table.shape), jnp.float32)]
+        + [pltpu.VMEM((4, 2, 2, r, h), low) for r, h in halves]
+        + [pltpu.VMEM((4, 2, 2, r, h), low) for r, h in halves]
+        + [pltpu.VMEM((4, 2, r, h), low) for r, h in halves]
+        + [pltpu.VMEM((4, r, h), low) for r, h in halves]
+        + [pltpu.VMEM((2, 4, r, h), low) for r, h in halves]
+        + [pltpu.VMEM((2, r // 2, h), jnp.float32) for r, h in halves]
+    )
+    dma = pltpu.SemaphoreType.DMA
+    return pl.pallas_call(
+        outbound_kernel,
+        out_shape=[
+            jax.ShapeDtypeStruct(result.shape, jnp.bfloat16),
+            jax.ShapeDtypeStruct(result.shape, jnp.float32),
+            jax.ShapeDtypeStruct(table.shape, jnp.float32),
+        ]
+        + [jax.ShapeDtypeStruct((2, r // 2, h), jnp.float32) for r, h in halves],
+        in_specs=vmem(9),
+        out_specs=vmem(7),
+        scratch_shapes=scratch
+        + [dma((PEERS,)), dma((PEERS,)), dma((PEERS,)), dma((PEERS,)), dma((2,)), dma((2, 5)), dma((8, 2, 5)), dma((2, 4))],
+        compiler_params=pltpu.CompilerParams(
+            collective_id=2, has_side_effects=True, vmem_limit_bytes=60 << 20
+        ),
+        name="outbound",
+    )(result, grads, home_line, slot_column, table, *locals_)
+
+
+def shard_halves(shard):
+    rows, columns = shard.shape
+    halves = shard.reshape(rows, 2, columns // 2).transpose(1, 0, 2)
+    return (rows, jnp.pad(halves, ((0, 0), (0, -rows % 16), (0, 0))))
+
+
+def chip_blocks(grad):
+    rows, columns = grad.shape
+    return grad.astype(jnp.bfloat16).reshape(4, 2, 2, rows // PEERS, columns)
+
+
+def joined(halves):
+    return jnp.concatenate([halves[0], halves[1]], axis=1)
+
+
 def per_device(
+    kernels,
     layer_in,
     out_grad,
     w_qkv,
@@ -184,19 +743,38 @@
     page_num = rows_dev // PAGE
     slot_of = token_slot[0]
     home_rows = home_index[0]
-    full_qkv, full_out, full_up, full_down, full_vec = (
-        lax.all_gather(w_qkv, ("regions", "shard"), axis=0, tiled=True),
-        lax.all_gather(w_out, ("regions", "shard"), axis=0, tiled=True),
-        lax.all_gather(w_up, ("regions", "shard"), axis=0, tiled=True),
-        lax.all_gather(w_down, ("regions", "shard"), axis=0, tiled=True),
-        lax.all_gather(vectors, ("regions", "shard"), axis=1, tiled=True),
-    )
+    if kernels:
+        beside = jnp.pad(vectors.T, ((0, 0), (0, VEC_COLS - vectors.shape[0])))
+        wide_qkv = jnp.concatenate([w_qkv, beside], axis=1)
+        slot_at = slot_of + slot_cap * (slot_of // slot_cap)
+        home_at = home_rows + slot_cap * (home_rows // slot_cap)
+        homed, cotangent, *fulls = inbound(
+            tokens,
+            out_grad[0],
+            slot_at[None],
+            home_at[:, None],
+            [shard_halves(shard) for shard in (wide_qkv, w_out, w_up, w_down)],
+        )
+        cotangent = cotangent.astype(jnp.float32)
+        full_qkv, full_out, full_up, full_down = [
+            full.reshape(-1, full.shape[4]) for full in fulls
+        ]
+        full_vec = full_qkv[:, 3 * model_dim : 3 * model_dim + vectors.shape[0]].T
+        full_qkv = full_qkv[:, : 3 * model_dim]
+    else:
+        full_qkv, full_out, full_up, full_down, full_vec = (
+            lax.all_gather(w_qkv, ("regions", "shard"), axis=0, tiled=True),
+            lax.all_gather(w_out, ("regions", "shard"), axis=0, tiled=True),
+            lax.all_gather(w_up, ("regions", "shard"), axis=0, tiled=True),
+            lax.all_gather(w_down, ("regions", "shard"), axis=0, tiled=True),
+            lax.all_gather(vectors, ("regions", "shard"), axis=1, tiled=True),
+        )
+        homed = exchange(tokens, slot_of, home_rows, groups, slot_cap).astype(jnp.bfloat16)
+        cotangent = exchange(out_grad[0], slot_of, home_rows, groups, slot_cap)
     vec_rows = full_vec.astype(jnp.float32)
     qkv_bias = jnp.concatenate([vec_rows[0], jnp.zeros_like(vec_rows[0]), vec_rows[1]])
     code_rows = position_codes(box_x[0].reshape(page_num, PAGE), box_y[0].reshape(page_num, PAGE))
     bias_mats = bias_table(relative)
-    homed = exchange(tokens, slot_of, home_rows, groups, slot_cap).astype(jnp.bfloat16)
-    cotangent = exchange(out_grad[0], slot_of, home_rows, groups, slot_cap)
     projected = (jnp.dot(homed, full_qkv, preferred_element_type=jnp.float32) + qkv_bias).astype(
         jnp.bfloat16
     )
@@ -247,8 +825,6 @@
     in_home = grad_one + jnp.einsum(
         "tf,df->td", grad_dense, full_qkv, preferred_element_type=jnp.float32
     )
-    layer_out = exchange(result.astype(jnp.bfloat16), home_rows, slot_of, groups, slot_cap)
-    in_grad = exchange(in_home.astype(jnp.bfloat16), home_rows, slot_of, groups, slot_cap)
     grad_vec = jnp.concatenate(
         [
             jnp.stack(
@@ -267,16 +843,42 @@
         ],
         axis=0,
     )
-    grad_qkv, grad_out, grad_up, grad_down, grad_vectors = (
-        lax.psum_scatter(grad_qkv.astype(jnp.bfloat16), ("regions", "shard"), scatter_dimension=0, tiled=True).astype(jnp.float32),
-        lax.psum_scatter(grad_out.astype(jnp.bfloat16), ("regions", "shard"), scatter_dimension=0, tiled=True).astype(jnp.float32),
-        lax.psum_scatter(grad_up.astype(jnp.bfloat16), ("regions", "shard"), scatter_dimension=0, tiled=True).astype(jnp.float32),
-        lax.psum_scatter(grad_down.astype(jnp.bfloat16), ("regions", "shard"), scatter_dimension=0, tiled=True).astype(jnp.float32),
-        lax.psum_scatter(grad_vec, ("regions", "shard"), scatter_dimension=1, tiled=True),
-    )
     mats_total = jnp.sum(mats_pages, axis=0)
     table_back = jax.vjp(bias_table, relative)[1]
-    grad_relative = lax.psum(table_back(mats_total)[0], ("regions", "shard"))
+    table_local = table_back(mats_total)[0]
+    if kernels:
+        beside = jnp.pad(grad_vec.T, ((0, 0), (0, VEC_COLS - grad_vec.shape[0])))
+        heads, entries = relative.shape
+        layer_out, in_grad, table_sum, *ends = outbound(
+            result.astype(jnp.bfloat16),
+            in_home.astype(jnp.bfloat16),
+            home_at[None],
+            slot_at[:, None],
+            jnp.pad(table_local, ((0, -heads % 8), (0, -entries % 128))),
+            [
+                chip_blocks(grad)
+                for grad in (
+                    jnp.concatenate([grad_qkv, beside], axis=1),
+                    grad_out,
+                    grad_up,
+                    grad_down,
+                )
+            ],
+        )
+        grad_relative = table_sum[:heads, :entries]
+        grad_qkv, grad_out, grad_up, grad_down = [joined(end) for end in ends]
+        grad_vectors = grad_qkv[:, 3 * model_dim : 3 * model_dim + vectors.shape[0]].T
+        grad_qkv = grad_qkv[:, : 3 * model_dim]
+    else:
+        layer_out = exchange(result.astype(jnp.bfloat16), home_rows, slot_of, groups, slot_cap)
+        in_grad = exchange(in_home.astype(jnp.bfloat16), home_rows, slot_of, groups, slot_cap)
+        over = ("regions", "shard")
+        grad_qkv, grad_out, grad_up, grad_down = [
+            lax.psum_scatter(grad, over, scatter_dimension=0, tiled=True)
+            for grad in (grad_qkv, grad_out, grad_up, grad_down)
+        ]
+        grad_vectors = lax.psum_scatter(grad_vec, over, scatter_dimension=1, tiled=True)
+        grad_relative = lax.psum(table_local, over)
     firsts_qkv, seconds_qkv, update_qkv = adam_step(
         w_qkv.astype(jnp.float32), grad_qkv, first_qkv, second_qkv, DECAY_RATE
     )
@@ -326,8 +928,9 @@
 
 
 def solution(mesh):
+    kernels = mesh.shape["regions"] == PEERS and mesh.shape["shard"] == 2
     return jax.shard_map(
-        per_device,
+        functools.partial(per_device, kernels),
         mesh=mesh,
         in_specs=(
             P("shard", "regions", None),

time: 815 us -> 648 us (0.80)
  waiting for transfers between devices: 408 us -> 0 us
  Pallas kernels: 0 us -> 402 us
  blocking collectives: 115 us -> 0 us
  matrix products: 178 us -> 144 us
  starting transfers between devices: 30.8 us -> 0 us
  local copies, waits for them, and re-layouts: 23 us -> 49.4 us
  between operations: 15.3 us -> 2.01 us
    pallas_call x0 -> x2, Pallas kernels: none -> 402 us  [the longest x1 204 us: inbound(): pl.pallas_call(inbound_kernel, out_shape=[jax.ShapeDtypeStruct(rows.shape...]
    reduce_scatter x4 -> x0, waiting for transfers between devices: 285 us -> none  [the longest x1 110 us: per_device(): lax.psum_scatter(grad_down.astype(jnp.bfloat16), ('regions', 'shard'), sc...]
    all_gather x4 -> x0, waiting for transfers between devices: 97.5 us -> none  [the longest x1 54.5 us: per_device(): lax.all_gather(w_up, ('regions', 'shard'), axis=0, tiled=True)]
    all_gather x1 -> x0, blocking collectives: 69.1 us -> none  [per_device(): lax.all_gather(vectors, ('regions', 'shard'), axis=1, tiled=True)]
    unnamed x1 -> x0, blocking collectives: 46.1 us -> none
    all_to_all x4 -> x0, starting transfers between devices: 30 us -> none  [exchange(): lax.all_to_all(packed.reshape(groups, slot_cap, rows.shape[1]), 'regions'...]
    dot_general x8 -> x1, matrix products: 31.3 us -> 6.49 us  [per_device(): jnp.einsum('tf,df->td', grad_dense, full_qkv, preferred_element_type=jnp....]
    all_to_all x4 -> x0, waiting for transfers between devices: 23.1 us -> none  [exchange(): lax.all_to_all(packed.reshape(groups, slot_cap, rows.shape[1]), 'regions'...]
  transfers between devices with their start and end apart: 12 -> 0, of which waited for: 6 -> 0; matrix products, arithmetic and copies ran while one was open for 22% -> 0% of each run, Pallas kernels for 0% -> 0%
where the time goes in v2:
time: 648 us; the launch traced here: 638 us
  Pallas kernels  402 us (62%)
  matrix products  144 us (22%)
  local copies, waits for them, and re-layouts  49.4 us (8%)
  other arithmetic  40.2 us (6%)
    pallas_call x1, Pallas kernels, inbound(): pl.pallas_call(inbound_kernel, out_shape=[jax.ShapeDtypeStruct(rows.shape...  204 us
    pallas_call x1, Pallas kernels, outbound(): pl.pallas_call(outbound_kernel, out_shape=[jax.ShapeDtypeStruct(result.sh...  198 us
    dot_general x1, matrix products, per_device(): jnp.dot(hidden_low, full_up, preferred_element_type=jnp.float32)  22.8 us

profile of v2, /device:TPU:0, one launch (start us, length us, event | category | flops | bytes accessed | tf_op | source)
XLA Modules:
  0.0 638.0 jit_solution(12678549710382402676)
XLA Ops:
  7.1 1.6 copy.147
  10.1 1.3 multiply_add_fusion.9.slot_line
  11.4 204.0 %inbound.1 = (bf16[576,768]{1,0:T(8,128)(2,1)}, bf16[576,768]{1,0:T(8,128)(2,1)}, bf16[4,2,2,48,2560]{4,3,2,1,0:T(8,128)(2,1)}, bf16[4,2,2,48,768]{4,3,2,1,0:T(8...) custom-call(bf16[576,768]{1,0:T(8,128)(2,1)} %bitcast.181, ...), custom_call_target="tpu_custom_call" | custom-call | tf_op jit(solution)/shard_map/inbound/pallas_call | solution.py:574
  217.1 6.0 add_convert_fusion.1
  223.2 4.1 copy.107
  230.2 1.5 reshape.471
  231.7 1.2 slice.174
  232.9 2.8 fusion.32
  235.7 11.2 %fusion.12 = f32[12,576,576]{1,2,0:T(8,128)} fusion(f32[12,128,576]{1,2,0:T(8,128)S(1)} %fusion.32, s32[576]{0:T(1024)S(1)} %get-tuple-element.246, s32[576]{0:T(1024)S(1)} %get-tuple-element.247, s32[576]{0:T(1024)S(1)} %add_select_fusion), kind=kOutput, calls=%fused_computation.34 | convolution fusion | flops 6115663872 | bytes 19471104 | tf_op jit(solution)/shard_map/while/body/eval_jaxpr/hpb,qb->hpq/dot_general | solution.py:58
  246.9 11.2 %fusion.84 = (f32[12,576]{1,0:T(8,128)S(1)}, f32[12,576,576]{1,2,0:T(8,128)}) fusion(f32[12,576,576]{1,2,0:T(8,128)} %fusion.12, bf16[576,3,12,64]{0,3,2,1:T(8,128)(2,1)S(1)} %bitcast.161), kind=kOutput, calls=%fused_computation.185 | convolution fusion | flops 521544960 | bytes 33844224 | tf_op jit(solution)/shard_map/while/body/eval_jaxpr/phd,qhd->hpq/dot_general | solution.py:66
  258.0 8.5 %fusion = f32[12,576]{1,0:T(8,128)S(1)} fusion(f32[12,576,576]{1,2,0:T(8,128)} %get-tuple-element.235, f32[12,576]{1,0:T(8,128)S(1)} %get-tuple-element.234), kind=kLoop, calls=%fused_computation.6 | loop fusion | flops 7955712 | bytes 15980544 | tf_op jit(solution)/shard_map/while/body/eval_jaxpr/reduce_sum | solution.py:76
  266.6 9.5 %fusion.28 = bf16[12,64,576]{2,1,0:T(8,128)(2,1)S(1)} fusion(f32[12,576,576]{1,2,0:T(8,128)} %get-tuple-element.235, f32[12,576]{1,0:T(8,128)S(1)} %fusion, f32[12,576]{1,0:T(8,128)S(1)} %get-tuple-element.234, bf16[576,3,12,64]{0,3,2,1:T(8,128)(2,1)S(1)} %bitcast.162), kind=kOutput, calls=%fused_computation.66 | convolution fusion | flops 521994240 | bytes 17874944 | tf_op jit(solution)/shard_map/while/body/eval_jaxpr/hpq,qhd->phd/dot_general | solution.py:78
  277.1 1.2 copy-done.2
  278.7 22.8 %multiply_convert_fusion.1 = (bf16[576,3072]{1,0:T(8,128)(2,1)S(1)}, f32[576,3072]{1,0:T(8,128)}, f32[576,3072]{1,0:T(8,128)}) fusion(f32[3072]{0:T(1024)S(1)} %add.337, bf16[768,3072]{1,0:T(8,128)(2,1)} %bitcast.204, f32[576,768]{1,0:T(8,128)} %copy-done.2, f32[768]{0:T(1024)S(1)} %get-tuple-element.182, f32[768]{0:T(1024)S(1)} %get-tuple-element.183, ...), kind=kOutput, calls=%fused_computation.14 | convolution fusion | flops 2836905984 | bytes 24205824 | tf_op jit(solution)/shard_map/dot_general | solution.py:791
  301.5 5.5 fusion.86
  307.4 2.2 fusion.23
  309.7 1.4 convert_reduce_fusion.1
  311.0 6.0 convolution_convert_fusion.1
  317.0 9.1 %fusion.87 = (bf16[3072]{0:T(1024)(128)(2,1)}, bf16[576,3072]{1,0:T(8,128)(2,1)S(1)}) fusion(f32[576,3072]{1,0:T(8,128)} %get-tuple-element.217, bf16[3072,768]{1,0:T(8,128)(2,1)S(1)} %bitcast.211, f32[576,768]{1,0:T(8,128)S(1)} %get-tuple-element.211, f32[576,3072]{1,0:T(8,128)} %get-tuple-element.238, f32[3072]{0:T(1024)S(1)} %add.337), kind=kOutput, calls=%fused_computation.188 | convolution fusion | flops 2746659840 | bytes 24201216 | tf_op jit(solution)/shard_map/td,fd->tf/dot_general | solution.py:803
  326.1 6.1 convolution_convert_fusion.2
  332.2 4.0 multiply_reduce_fusion.1
  336.2 1.2 convert_reduce_fusion
  337.4 2.2 convolution_convert_fusion.3
  339.6 1.8 convolution_convert_fusion.4
  341.4 2.2 copy.109
  343.6 11.7 %multiply_reduce_fusion = (f32[12,576]{1,0:T(8,128)S(1)}, f32[12,576,576]{1,2,0:T(8,128)}) fusion(f32[12,576,576]{1,2,0:T(8,128)} %get-tuple-element.235, f32[12,576]{1,0:T(8,128)S(1)} %log_add_fusion, bf16[576,12,64]{0,2,1:T(8,128)(2,1)} %bitcast.166, bf16[576,3,12,64]{0,3,2,1:T(8,128)(2,1)S(1)} %bitcast.163), kind=kOutput, calls=%fused_computation.1 | convolution fusion | flops 521544960 | bytes 33786880 | tf_op jit(solution)/shard_map/while/body/eval_jaxpr/phd,qhd->hpq/dot_general | solution.py:89
  355.3 12.2 %multiply_convert_fusion = bf16[12,576,576]{1,2,0:T(8,128)(2,1)S(1)} fusion(f32[12,576,576]{1,2,0:T(8,128)} %get-tuple-element.243, f32[12,576,576]{1,2,0:T(8,128)} %get-tuple-element.235, f32[12,576]{1,0:T(8,128)S(1)} %get-tuple-element.242, f32[12,576]{1,0:T(8,128)S(1)} %log_add_fusion), kind=kLoop, calls=%fused_computation | loop fusion | flops 15925248 | bytes 39868416 | tf_op jit(solution)/shard_map/while/body/eval_jaxpr/convert_element_type | solution.py:93
  367.6 1.7 multiply_bitcast_fusion.1
  369.3 1.8 copy-done
  371.0 2.7 multiply_bitcast_fusion
  373.7 8.8 %fusion.24 = bf16[576,1,12,64]{0,3,2,1:T(8,128)(2,1)S(1)} fusion(bf16[576,12,64]{0,2,1:T(8,128)(2,1)S(1)} %bitcast.167, f32[12,576,576]{1,2,0:T(8,128)} %get-tuple-element.235, f32[12,576]{1,0:T(8,128)S(1)} %log_add_fusion), kind=kOutput, calls=%fused_computation.62 | convolution fusion | flops 517570560 | bytes 17722368 | tf_op jit(solution)/shard_map/while/body/eval_jaxpr/hpq,phd->qhd/dot_general | solution.py:88
  382.6 1.9 fusion.79
  384.5 1.5 copy.116
  386.0 5.1 convolution_convert_fusion
  393.8 1.3 stack.55
  395.1 1.3 stack.56
  397.0 1.3 stack.57
  398.3 1.3 stack.59
  399.5 1.3 stack.58
  400.8 2.0 concatenate.31
  402.8 1.6 copy.136
  405.4 2.4 pad_maximum_fusion.g_qkv
  407.8 6.6 %fusion.48 = f32[12,576,128]{2,1,0:T(8,128)S(1)} fusion(bf16[12,576,576]{1,2,0:T(8,128)(2,1)} %copy-done, s32[576]{0:T(1024)S(1)} %copy-done.25, s32[576]{0:T(1024)S(1)} %copy-done.27, s32[576]{0:T(1024)S(1)} %copy-done.29), kind=kOutput, calls=%fused_computation.108 | convolution fusion | flops 1019731968 | bytes 11508480 | tf_op jit(solution)/shard_map/while/body/eval_jaxpr/hpq,qb->hpb/dot_general | solution.py:101
  414.4 1.8 convolution_bitcast_fusion
  418.6 6.5 %add_convert_fusion.2.grad_ref = bf16[576,768]{1,0:T(8,128)(2,1)} fusion(f32[576,768]{1,0:T(8,128)S(1)} %copy-done.6, bf16[576,2304]{0,1:T(8,128)(2,1)} %bitcast.171, bf16[768,2560]{1,0:T(8,128)(2,1)} %bitcast.203), kind=kOutput, calls=%fused_computation.51 | convolution fusion | flops 2039316480 | bytes 9142272 | tf_op jit(solution)/shard_map/tf,df->td/dot_general | solution.py:825
  426.8 198.5 %outbound.1 = (bf16[576,768]{1,0:T(8,128)(2,1)}, f32[576,768]{1,0:T(8,128)}, f32[16,256]{1,0:T(8,128)}, f32[2,24,1280]{2,1,0:T(8,128)}, f32[2,24,384]{2,1,0:T(8,...) custom-call(bf16[576,768]{1,0:T(8,128)(2,1)} %get-tuple-element.218.result_ref, ...), custom_call_target="tpu_custom_call" | custom-call | tf_op jit(solution)/shard_map/outbound/pallas_call | solution.py:677
  627.7 1.1 slice_bitcast_fusion.12
  636.3 1.2 copy.154
  (203 shorter events, 32.3 us)
Async XLA Ops:
  223.1 4.1 copy-start.42
  223.1 4.1 copy-start.43
  223.2 4.2 copy-start.22
  223.2 6.7 %copy-start.44 = (pred[128]{0:T(512)(128)(4,1)S(1)}, pred[128]{0:T(512)(128)(4,1)}, u32[]{:S(2)}) copy-start(pred[128]{0:T(512)(128)(4,1)} %constant.67.clone.1) | copy-start | bytes 388
  227.3 8.4 %copy-start.24 = (s32[576]{0:T(1024)}, s32[576]{0:T(1024)S(1)}, u32[]{:S(2)}) copy-start(s32[576]{0:T(1024)S(1)} %get-tuple-element.246) | copy-start | bytes 6916
  227.3 8.4 %copy-start.26 = (s32[576]{0:T(1024)}, s32[576]{0:T(1024)S(1)}, u32[]{:S(2)}) copy-start(s32[576]{0:T(1024)S(1)} %get-tuple-element.247) | copy-start | bytes 6916
  227.4 8.3 %copy-start.28 = (s32[576]{0:T(1024)}, s32[576]{0:T(1024)S(1)}, u32[]{:S(2)}) copy-start(s32[576]{0:T(1024)S(1)} %add_select_fusion) | copy-start | bytes 6916
  266.5 9.5 %copy-start.8 = (bf16[576,768]{1,0:T(8,128)(2,1)S(1)}, bf16[576,768]{1,0:T(8,128)(2,1)}, u32[]{:S(2)}) copy-start(bf16[576,768]{1,0:T(8,128)(2,1)} %get-tuple-element.81) | copy-start | bytes 2654212
  266.5 9.5 %copy-start.41 = (f32[768]{0:T(1024)S(1)}, f32[768]{0:T(1024)}, u32[]{:S(2)}) copy-start(f32[768]{0:T(1024)} %get-tuple-element.184) | copy-start | bytes 9220
  266.6 9.5 %copy-start.45 = (bf16[4,2,2,48,768]{4,3,2,1,0:T(8,128)(2,1)S(1)}, bf16[4,2,2,48,768]{4,3,2,1,0:T(8,128)(2,1)}, u32[]{:S(2)}) copy-start(bf16[4,2,2,48,768]{4,3,2,1,0:T(8,128)(2,1)} %get-tuple-element.83) | copy-start | bytes 3538948
  278.7 22.8 %copy-start.3 = (f32[576,768]{1,0:T(8,128)S(1)}, f32[576,768]{1,0:T(8,128)}, u32[]{:S(2)}) copy-start(f32[576,768]{1,0:T(8,128)} %copy-done.2) | copy-start | bytes 5308420
  301.5 5.9 copy-start.4
  307.4 9.6 %slice-start.2 = ((s8[4718592]{0:T(1024)(128)(4,1)}), s8[4194304]{0:T(1024)(128)(4,1)S(1)}, s32[]{:S(2)}) async-start(s8[4718592]{0:T(1024)(128)(4,1)} %bitcast.209), calls=%async_computation.2 | async-start | bytes 8388608
  311.0 6.0 slice-start.3
  311.0 21.2 %slice-start = ((s8[4718592]{0:T(1024)(128)(4,1)}), s8[4194304]{0:T(1024)(128)(4,1)S(1)}, s32[]{:S(2)}) async-start(s8[4718592]{0:T(1024)(128)(4,1)} %bitcast.205), calls=%async_computation | async-start | bytes 8388608
  317.0 15.2 %slice-start.1 = ((s8[4718592]{0:T(1024)(128)(4,1)}), s8[524288]{0:T(1024)(128)(4,1)S(1)}, s32[]{:S(2)}) async-start(s8[4718592]{0:T(1024)(128)(4,1)} %bitcast.205), calls=%async_computation.1 | async-start | bytes 1048576
  336.2 3.4 copy-start.46
  367.6 3.5 copy-start
  371.0 2.7 copy-start.1
  405.4 2.4 copy-start.25
  405.4 2.4 copy-start.27
  405.4 2.4 copy-start.29
  416.2 2.4 copy-start.6
  418.6 6.5 %copy-start.33 = (s32[1,576]{1,0:T(1,128)S(1)}, s32[1,576]{1,0:T(1,128)}, u32[]{:S(2)}) copy-start(s32[1,576]{1,0:T(1,128)} %param.44) | copy-start | bytes 6916
  418.6 7.6 %copy-start.34 = (s32[1,576]{1,0:T(1,128)S(1)}, s32[1,576]{1,0:T(1,128)}, u32[]{:S(2)}) copy-start(s32[1,576]{1,0:T(1,128)} %param.45) | copy-start | bytes 6916
  426.8 199.8 %copy-start.11 = (bf16[96,768]{1,0:T(8,128)(2,1)S(1)}, bf16[96,768]{1,0:T(8,128)(2,1)}, u32[]{:S(2)}) copy-start(bf16[96,768]{1,0:T(8,128)(2,1)} %param.29) | copy-start | bytes 442372
  426.8 199.8 %copy-start.14 = (f32[96,768]{1,0:T(8,128)S(1)}, f32[96,768]{1,0:T(8,128)}, u32[]{:S(2)}) copy-start(f32[96,768]{1,0:T(8,128)} %param.39) | copy-start | bytes 884740
  426.8 199.8 %copy-start.15 = (f32[96,768]{1,0:T(8,128)S(1)}, f32[96,768]{1,0:T(8,128)}, u32[]{:S(2)}) copy-start(f32[96,768]{1,0:T(8,128)} %param.38) | copy-start | bytes 884740
  426.8 202.1 %copy-start.12 = (bf16[24,3072]{1,0:T(8,128)(2,1)S(1)}, bf16[24,3072]{1,0:T(8,128)(2,1)}, u32[]{:S(2)}) copy-start(bf16[24,3072]{1,0:T(8,128)(2,1)} %param.28) | copy-start | bytes 442372
  426.8 202.1 %copy-start.16 = (f32[24,3072]{1,0:T(8,128)S(1)}, f32[24,3072]{1,0:T(8,128)}, u32[]{:S(2)}) copy-start(f32[24,3072]{1,0:T(8,128)} %param.37) | copy-start | bytes 884740
  426.8 202.1 %copy-start.17 = (f32[24,3072]{1,0:T(8,128)S(1)}, f32[24,3072]{1,0:T(8,128)}, u32[]{:S(2)}) copy-start(f32[24,3072]{1,0:T(8,128)} %param.36) | copy-start | bytes 884740
  625.3 4.7 copy-start.32
  625.3 4.7 copy-start.21
  625.3 4.7 copy-start.30
  625.3 4.7 copy-start.31
  625.4 5.4 copy-start.18
  625.4 5.4 copy-start.13
  625.4 5.4 copy-start.19
  625.4 5.4 copy-start.20
  626.6 5.2 copy-start.39
  626.6 5.3 copy-start.40
  626.6 5.3 copy-start.35
  626.6 8.1 %copy-start.23 = (f32[12,253]{1,0:T(8,128)S(1)}, f32[12,253]{1,0:T(8,128)}, u32[]{:S(2)}) copy-start(f32[12,253]{1,0:T(8,128)} %param.31) | copy-start | bytes 36436
  626.6 8.1 %copy-start.36 = (f32[12,253]{1,0:T(8,128)S(1)}, f32[12,253]{1,0:T(8,128)}, u32[]{:S(2)}) copy-start(f32[12,253]{1,0:T(8,128)} %param.43) | copy-start | bytes 36436
  626.6 8.1 %copy-start.37 = (f32[12,253]{1,0:T(8,128)S(1)}, f32[12,253]{1,0:T(8,128)}, u32[]{:S(2)}) copy-start(f32[12,253]{1,0:T(8,128)} %param.42) | copy-start | bytes 36436
  626.6 8.1 %copy-start.38 = (f32[16,256]{1,0:T(8,128)S(1)}, f32[16,256]{1,0:T(8,128)}, u32[]{:S(2)}) copy-start(f32[16,256]{1,0:T(8,128)} %get-tuple-element.93) | copy-start | bytes 49156
  626.6 8.8 %copy-start.10 = (bf16[576,768]{1,0:T(8,128)(2,1)S(1)}, bf16[576,768]{1,0:T(8,128)(2,1)}, u32[]{:S(2)}) copy-start(bf16[576,768]{1,0:T(8,128)(2,1)} %get-tuple-element.87) | copy-start | bytes 2654212
  627.7 8.6 %copy-start.7 = (f32[576,768]{1,0:T(8,128)S(1)}, f32[576,768]{1,0:T(8,128)}, u32[]{:S(2)}) copy-start(f32[576,768]{1,0:T(8,128)} %get-tuple-element.88) | copy-start | bytes 5308420
  (5 other events, 7.6 us)

commit v3 on v2

--- a/solution.py
+++ b/solution.py
@@ -1,4 +1,3 @@
-import functools
 import jax
 import jax.numpy as jnp
 import numpy as np
@@ -153,6 +152,147 @@
     return (moment_new, square_new, update)
 
 
+ROWS = 576
+
+
+def softly(scores, axis):
+    peak = jnp.max(scores, axis=axis, keepdims=True)
+    raised = jnp.exp(scores - peak)
+    return raised * (1.0 / jnp.sum(raised, axis=axis, keepdims=True))
+
+
+def head_lift(tables, codes, h):
+    lines = tables[h]
+    lane = lax.broadcasted_iota(jnp.int32, (64, 128), 1)
+
+    def spread(n, size, low, high):
+        line = jnp.broadcast_to(lines[n : n + 1], (size, 128))
+        turned = pltpu.roll(line, 0, 1, stride=1, stride_axis=0)
+        return jnp.where((lane[:size] >= low) & (lane[:size] < high), turned, 0.0)
+
+    table = jnp.concatenate(
+        [spread(0, 64, 0, 64), spread(1, 32, 64, 96), spread(2, 32, 96, 128)], axis=0
+    )
+    high = table.astype(jnp.bfloat16)
+    low = (table - high.astype(jnp.float32)).astype(jnp.bfloat16)
+    both = jnp.concatenate([high, low], axis=1)
+    return jnp.dot(codes, both, preferred_element_type=jnp.float32).astype(jnp.bfloat16)
+
+
+def lane_mask(rows, h):
+    lane = lax.broadcasted_iota(jnp.int32, (rows, 128), 1)
+    return (lane < 64) if h == 0 else (lane >= 64)
+
+
+def pair_columns(qkv, pair):
+    width = qkv.shape[1] // 3
+    at = [pl.multiple_of(n * width + pair * 128, 128) for n in range(3)]
+    return [qkv[:, pl.ds(a, 128)] for a in at]
+
+
+NT = (((1,), (1,)), ((), ()))
+TN = (((0,), (0,)), ((), ()))
+
+
+def attend_pair(pair, qkv, tables, codes_ref, context):
+    count = qkv.shape[0]
+    codes = codes_ref[...]
+    queries, keys, values = pair_columns(qkv, pair)
+    right = jnp.concatenate([keys, codes, codes], axis=1)
+    scaled = queries * jnp.bfloat16(0.125)
+    results = []
+    for h in range(2):
+        mine = jnp.where(lane_mask(count, h), scaled, jnp.zeros_like(scaled))
+        left = jnp.concatenate([mine, head_lift(tables, codes, 2 * pair + h)], axis=1)
+        parts = []
+        for r in range(0, count, ROWS):
+            scores = lax.dot_general(left[r : r + ROWS], right, NT, preferred_element_type=jnp.float32)
+            weights = softly(scores, 1).astype(jnp.bfloat16)
+            parts.append(jnp.dot(weights, values, preferred_element_type=jnp.float32))
+        results.append(parts)
+    for n, r in enumerate(range(0, count, ROWS)):
+        both = jnp.where(lane_mask(ROWS, 0), results[0][n], results[1][n])
+        context[pl.ds(r, ROWS), pl.ds(pl.multiple_of(pair * 128, 128), 128)] = both.astype(jnp.bfloat16)
+
+
+def attend_pair_back(pair, qkv, grad_ref, tables, codes_ref, flipped_ref, grad_qkv, grad_tables):
+    count = qkv.shape[0]
+    width = qkv.shape[1] // 3
+    codes = codes_ref[...]
+    queries, keys, values = pair_columns(qkv, pair)
+    grads = grad_ref[:, pl.ds(pl.multiple_of(pair * 128, 128), 128)]
+    left = jnp.concatenate([keys, codes, codes], axis=1)
+    near = jnp.concatenate([keys, codes], axis=1)
+    scaled = queries * jnp.bfloat16(0.125)
+    out_q, out_k, out_v = [], [], []
+    for h in range(2):
+        mask = lane_mask(count, h)
+        mine = jnp.where(mask, scaled, jnp.zeros_like(scaled))
+        mine_grad = jnp.where(mask, grads, jnp.zeros_like(grads))
+        right = jnp.concatenate([mine, head_lift(tables, codes, 2 * pair + h)], axis=1)
+        total = None
+        k_parts, v_parts = [], []
+        if True:
+            scores = lax.dot_general(left, right, NT, preferred_element_type=jnp.float32)
+            chances = softly(scores, 0)
+            grad_chances = lax.dot_general(values, mine_grad, NT, preferred_element_type=jnp.float32)
+            inner = jnp.sum(chances * grad_chances, axis=0, keepdims=True)
+            grad_scores = (chances * (grad_chances - inner)).astype(jnp.bfloat16)
+            v_rows = jnp.dot(chances.astype(jnp.bfloat16), grads, preferred_element_type=jnp.float32)
+            k_rows = jnp.dot(grad_scores, queries, preferred_element_type=jnp.float32)
+            total = lax.dot_general(grad_scores, near, TN, preferred_element_type=jnp.float32)
+        out_q.append(total[:, :128])
+        out_k.append(k_rows)
+        out_v.append(v_rows)
+        partial = total[:, 128:]
+        high = partial.astype(jnp.bfloat16)
+        low = (partial - high.astype(jnp.float32)).astype(jnp.bfloat16)
+        mats = lax.dot_general(
+            flipped_ref[...], jnp.concatenate([high, low], axis=1), TN, preferred_element_type=jnp.float32
+        )
+        mats = mats[:, :128] + mats[:, 128:]
+        lane = lax.broadcasted_iota(jnp.int32, (64, 128), 1)
+
+        def gathered(row, size, low_lane, high_lane):
+            part = jnp.where((lane[:size] >= low_lane) & (lane[:size] < high_lane), mats[row : row + size], 0.0)
+            turned = pltpu.roll(part, 0, 1, stride=1, stride_axis=0)
+            return jnp.sum(turned, axis=0, keepdims=True)
+
+        grad_tables[2 * pair + h] = jnp.concatenate(
+            [
+                gathered(0, 64, 0, 64),
+                gathered(64, 32, 64, 96),
+                gathered(96, 32, 96, 128),
+                jnp.zeros((5, 128), jnp.float32),
+            ],
+            axis=0,
+        )
+    mask = lane_mask(count, 0)
+    for n, (parts, factor) in enumerate(((out_q, 0.125), (out_k, 0.125), (out_v, 1.0))):
+        both = jnp.where(mask, parts[0], parts[1]) * factor
+        grad_qkv[:, pl.ds(pl.multiple_of(n * width + pair * 128, 128), 128)] = both.astype(jnp.bfloat16)
+
+
+def code_columns(seq, box_x, box_y):
+    columns = jnp.arange(128, dtype=jnp.int32)[None]
+    hit = (columns == seq[:, None]) | (columns == 64 + box_x[:, None]) | (columns == 96 + box_y[:, None])
+    return hit.astype(jnp.bfloat16)
+
+
+def table_lines(relative):
+    seq = jnp.pad(relative[:, :127], ((0, 0), (0, 1)))
+    horizontal = jnp.pad(relative[:, 127:190], ((0, 0), (0, 65)))
+    vertical = jnp.pad(relative[:, 190:253], ((0, 0), (0, 65)))
+    lines = [jnp.roll(seq, -63, 1), jnp.roll(horizontal, 33, 1), jnp.roll(vertical, 65, 1)]
+    return jnp.pad(jnp.stack(lines, axis=1), ((0, 0), (0, 5), (0, 0)))
+
+
+def lines_back(grad):
+    return jnp.concatenate(
+        [grad[:, 0, :127], grad[:, 1, 64:127], jnp.roll(grad[:, 2], -96, 1)[:, :63]], axis=1
+    )
+
+
 MESH = pl.DeviceIdType.MESH
 PEERS = 16
 VEC_COLS = 256
@@ -188,29 +328,28 @@
         self.send, self.recv, self.local = send, recv, local
         self.slots, self.half = packed.shape[1], packed.shape[2]
 
-    def pack(self, rows, row_of):
+    def pack(self, rows, row_of, groups=range(4)):
+        self.pack_value(rows[...], row_of, groups)
+
+    def pack_value(self, rows, row_of, groups=range(4)):
+        span = 4 * self.slots
         left, right = rows[:, : self.half], rows[:, self.half :]
-
-        def one(k, carry):
-            d = self.me ^ k
-            base = d * self.slots
-            at = lax.broadcasted_iota(jnp.int32, (self.slots, rows.shape[0]), 0) + base
+        shift = self.slots // 2
+        for j in groups:
+            group = lax.div(self.me, 4) ^ j
+            at = lax.broadcasted_iota(jnp.int32, (span, rows.shape[0]), 0) + group * span
             target = row_of[...]
             lefts = jnp.where(at == target, 1.0, 0.0).astype(jnp.bfloat16)
-            rights = jnp.where(at == target + self.slots // 2, 1.0, 0.0).astype(jnp.bfloat16)
+            rights = jnp.where(at == target + shift, 1.0, 0.0).astype(jnp.bfloat16)
             block = jnp.dot(lefts, left, preferred_element_type=jnp.float32) + jnp.dot(
                 rights, right, preferred_element_type=jnp.float32
             )
-            self.packed[d] = block.astype(jnp.bfloat16)
-
-            @pl.when(k > 0)
-            def _():
-                self.copy(k).start()
-
-            return carry
-
-        lax.fori_loop(0, PEERS, one, 0)
-        self.own().start()
+            self.packed[pl.ds(4 * group, 4)] = block.astype(jnp.bfloat16).reshape(4, self.slots, self.half)
+            for k in range(4):
+                if j + k:
+                    self.copy(4 * j + k).start()
+                else:
+                    self.own().start()
 
     def copy(self, k):
         d = self.me ^ k
@@ -245,14 +384,21 @@
 
 
 def pieces_of(rows, half):
-    if rows % 32 == 0:
-        return [(0, rows // 2, 0, half, True), (rows // 2, rows // 2, 0, half, False)]
-    cut = (half // 128 + 1) // 2 * 128
-    return [(0, rows, 0, cut, True), (0, rows, cut, half - cut, False)]
+    tiles = half // 128
+    if rows % 64 == 0:
+        cuts = [(n * rows // 4, rows // 4, 0, half) for n in range(4)]
+    elif tiles < 4:
+        wide = (tiles + 1) // 2 * 128
+        cuts = [(0, rows, 0, wide), (0, rows, wide, half - wide)]
+    else:
+        ends = [0, (tiles + 3) // 4, tiles // 2, tiles - (tiles + 3) // 4, tiles]
+        cuts = [(0, rows, 128 * ends[n], 128 * (ends[n + 1] - ends[n])) for n in range(4)]
+    return [[(*cuts[n], True), (*cuts[n + 1], False)] for n in range(0, len(cuts), 2)]
 
 
 class Gather:
-    STAGES = 7
+    TIGHT = (0, 1, 2, 3, 4, 5, 6)
+    OFFSETS = (0, 1, 2, 4, 6, 8, 10)
 
     def __init__(self, where, whole, piece, sems):
         self.where, self.whole, self.piece, self.sems = where, whole, piece, sems
@@ -304,14 +450,19 @@
         me, core, z, y, x = self.where
         x_first = self.piece[4]
         every = slice(None)
-        if n == 2:
-            ref, device = self.part(every, every, every), (me, 1 - core)
-        elif n == 0:
+        other = (me, 1 - core)
+        if n == 0:
             ref, device = self.part(every, y, x), (me ^ (1 if x_first else 2), core)
-        elif x_first:
+        elif n == 1 and x_first:
             ref, device = self.part(every, y, every), (me ^ 2, core)
+        elif n == 1:
+            ref, device = self.part(every, every, x), (me ^ 1, core)
+        elif n == 2:
+            ref, device = self.part(every, y, x), other
+        elif n == 3:
+            ref, device = (self.part(every, y, 1 - x) if x_first else self.part(every, 1 - y, x)), other
         else:
-            ref, device = self.part(every, every, x), (me ^ 1, core)
+            ref, device = (self.part(every, 1 - y, every) if x_first else self.part(every, every, 1 - x)), other
         return remote(ref, ref, self.sems.at[0, 6 + n], self.sems.at[1, 6 + n], device)
 
     def run(self, stage):
@@ -322,26 +473,32 @@
         elif stage == 3:
             self.z_waits(2)
             self.plane(0).start()
-        elif stage < 6:
-            self.plane(stage - 4).wait_recv()
-            self.plane(stage - 3).start()
+            self.plane(2).start()
+        elif stage == 4:
+            self.plane(0).wait_recv()
+            self.plane(1).start()
+            self.plane(3).start()
+        elif stage == 5:
+            self.plane(1).wait_recv()
+            self.plane(4).start()
         else:
-            self.plane(2).wait_recv()
+            for n in (2, 3, 4):
+                self.plane(n).wait_recv()
 
     def sent(self):
         for t in range(3):
             self.z_sends(t, lambda copy: copy.wait_send())
-        for n in range(3):
+        for n in range(5):
             self.plane(n).wait_send()
 
 
 class Scatter:
-    STAGES = 9
-
-    def __init__(self, where, local, sums, from_core, from_near, from_far, from_z, piece, sems):
+    OFFSETS = (0, 2, 4, 6, 8, 10, 12)
+
+    def __init__(self, where, local, sums, from_core, from_near, from_far, from_z, fetch, piece, sems):
         self.where, self.local, self.sums, self.piece, self.sems = where, local, sums, piece, sems
         self.from_core, self.from_near, self.from_far, self.from_z = from_core, from_near, from_far, from_z
-        self.half = sums.shape[4]
+        self.half, self.fetch = sums.shape[4], fetch
 
     def cut(self, ref, *lead, core=None):
         r0, rows, c0, cols, _ = self.piece
@@ -354,6 +511,11 @@
         src = self.cut(self.local, every, every, every, core=1 - core)
         dst = self.cut(self.from_core, every, every, every)
         return remote(src, dst, self.sems.at[0, 0], self.sems.at[1, 0], (me, 1 - core))
+
+    def own_half(self):
+        every = slice(None)
+        src = self.cut(self.local, every, every, every, core=self.where[1])
+        return pltpu.make_async_copy(src, self.cut(self.sums, every, every, every), self.fetch)
 
     def near(self):
         me, core, z, y, x = self.where
@@ -398,14 +560,14 @@
         me, core, z, y, x = self.where
         if stage == 0:
             self.between_cores().start()
+            self.own_half().start()
         elif stage == 1:
+            self.own_half().wait()
             self.between_cores().wait_recv()
 
             def one(i, carry):
                 a, b, c = lax.div(i, 4), lax.div(lax.rem(i, 4), 2), lax.rem(i, 2)
-                mine = self.cut(self.local, a, b, c, core=core)[...].astype(jnp.float32)
-                other = self.cut(self.from_core, a, b, c)[...].astype(jnp.float32)
-                self.cut(self.sums, a, b, c)[...] = (mine + other).astype(jnp.bfloat16)
+                self.add(self.cut(self.sums, a, b, c), self.cut(self.from_core, a, b, c))
                 return carry
 
             lax.fori_loop(0, 16, one, 0)
@@ -487,18 +649,23 @@
                     self.along_z(sender, True).wait_send()
 
 
-def staggered(tasks, stages, extra=None):
-    for k in range(len(tasks) + stages - 1):
-        for i, task in enumerate(tasks):
-            if 0 <= k - i < stages:
-                task.run(k - i)
-        if extra is not None:
-            extra(k)
+def stepper(tasks):
+    def step(k):
+        for pair, first, offsets in tasks:
+            if k - first in offsets:
+                for task in pair:
+                    task.run(offsets.index(k - first))
+
+    return step, max(first + offsets[-1] for _, first, offsets in tasks) + 1
+
+
+PAIRS = 6
+READY = 8
 
 
 def inbound_kernel(
-    rows_ref, grad_ref, slot_line, home_column, s_qkv, s_out, s_up, s_down,
-    homed, cotangent, w_qkv, w_out, w_up, w_down,
+    rows_ref, grad_ref, slot_line, home_column, tables, codes, s_qkv, s_out, s_up, s_down,
+    homed, cotangent, qkv, context, vec_rows, w_qkv, w_out, w_up, w_down,
     packed_a, arrived_a, packed_b, arrived_b, p_qkv, p_out, p_up, p_down, b_qkv, b_out, b_up, b_down,
     send_a, recv_a, send_b, recv_b, local_sems, pair_sems, block_sems, piece_sems,
 ):
@@ -517,7 +684,6 @@
         pair.start()
     moved = Exchange(where, packed_a, arrived_a, send_a, recv_a, local_sems.at[0])
     moved_grad = Exchange(where, packed_b, arrived_b, send_b, recv_b, local_sems.at[1])
-    moved.pack(rows_ref, slot_line)
     placed = []
     tasks = []
     for i in range(4):
@@ -537,61 +703,210 @@
         placed.append(copy)
     for i in range(4):
         placed[i].wait()
-        for piece in pieces_of(blocks[i].shape[0], blocks[i].shape[1]):
+        for pair in pieces_of(blocks[i].shape[0], blocks[i].shape[1]):
             n = len(tasks)
-            tasks.append(Gather(where, wholes[i], piece, piece_sems.at[n]))
-
-    def extra(k):
-        if k == 2:
-            moved_grad.pack(grad_ref, slot_line)
-
-    staggered(tasks, Gather.STAGES, extra)
+            pair = [Gather(where, wholes[i], piece, piece_sems.at[2 * n + j]) for j, piece in enumerate(pair)]
+            tasks.append((pair, n, Gather.TIGHT if i == 0 else Gather.OFFSETS))
+    step, steps = stepper(tasks)
+
+    step(0)
+    moved.pack(rows_ref, slot_line)
+    for k in range(1, READY):
+        step(k)
     moved.wait()
     moved.unpack(home_column, homed, jnp.bfloat16)
+    moved_grad.pack(grad_ref, slot_line)
+    width = homed.shape[1]
+    columns = w_qkv[:, :, :, :, 3 * width : 3 * width + 128].reshape(width, 128)
+    vec_rows[...] = columns.astype(jnp.float32).T[: vec_rows.shape[0]]
+    for n in range(3):
+        part = w_qkv[:, :, :, :, n * width : (n + 1) * width].reshape(width, width)
+        projected = jnp.dot(homed[...], part, preferred_element_type=jnp.float32)
+        if n != 1:
+            projected = projected + vec_rows[n // 2 : n // 2 + 1]
+        qkv[:, n * width : (n + 1) * width] = projected.astype(jnp.bfloat16)
+
+    def one(pair, carry):
+        attend_pair(pair, qkv, tables, codes, context)
+        for j in range(PAIRS):
+
+            @pl.when(pair == j)
+            def _(j=j):
+                step(READY + j)
+
+        return carry
+
+    lax.fori_loop(0, PAIRS, one, 0)
+    for k in range(READY + PAIRS, steps):
+        step(k)
     moved_grad.wait()
     moved_grad.unpack(home_column, cotangent, jnp.bfloat16)
     for pair in pairs:
         pair.wait_send()
-    for task in tasks:
-        task.sent()
+    for pair, _, _ in tasks:
+        for task in pair:
+            task.sent()
 
 
 def vmem(count):
     return [pl.BlockSpec(memory_space=pltpu.VMEM)] * count
 
 
-def inbound(rows, grads, slot_line, home_column, shards):
+def inbound(rows, grads, slot_line, home_column, tables, codes, shards):
     tokens, width = rows.shape
     slots = 2 * (2 * tokens // PEERS)
-    buffer = pltpu.VMEM((PEERS, slots, width // 2), jnp.bfloat16)
+    low = jnp.bfloat16
+    buffer = pltpu.VMEM((PEERS, slots, width // 2), low)
     wholes, pair_shapes, block_shapes = [], [], []
     for shard, padded in shards:
         half = padded.shape[2]
-        wholes.append(jax.ShapeDtypeStruct((4, 2, 2, 2 * shard, 2 * half), jnp.bfloat16))
-        pair_shapes.append(pltpu.VMEM(padded.shape[1:], jnp.bfloat16))
-        block_shapes.append(pltpu.VMEM((2 * shard, half), jnp.bfloat16))
+        wholes.append(jax.ShapeDtypeStruct((4, 2, 2, 2 * shard, 2 * half), low))
+        pair_shapes.append(pltpu.VMEM(padded.shape[1:], low))
+        block_shapes.append(pltpu.VMEM((2 * shard, half), low))
     dma = pltpu.SemaphoreType.DMA
     return pl.pallas_call(
         inbound_kernel,
-        out_shape=[jax.ShapeDtypeStruct(rows.shape, jnp.bfloat16)] * 2 + wholes,
-        in_specs=vmem(8),
-        out_specs=vmem(6),
+        out_shape=[
+            jax.ShapeDtypeStruct((tokens, width), low),
+            jax.ShapeDtypeStruct((tokens, width), low),
+            jax.ShapeDtypeStruct((tokens, 3 * width), low),
+            jax.ShapeDtypeStruct((tokens, width), low),
+            jax.ShapeDtypeStruct((16, width), jnp.float32),
+        ]
+        + wholes,
+        in_specs=vmem(10),
+        out_specs=vmem(9),
         scratch_shapes=[buffer] * 4 + pair_shapes + block_shapes
-        + [dma((PEERS,)), dma((PEERS,)), dma((PEERS,)), dma((PEERS,)), dma((2,)), dma((2, 4)), dma((4,)), dma((8, 2, 9))],
+        + [dma((PEERS,)), dma((PEERS,)), dma((PEERS,)), dma((PEERS,)), dma((2,)), dma((2, 4)), dma((4,)), dma((14, 2, 11))],
         compiler_params=pltpu.CompilerParams(
             collective_id=1, has_side_effects=True, vmem_limit_bytes=60 << 20
         ),
         name="inbound",
-    )(rows, grads, slot_line, home_column, *[padded for _, padded in shards])
+    )(rows, grads, slot_line, home_column, tables, codes, *[padded for _, padded in shards])
+
+
+def normed_rows(rows):
+    centre = rows - jnp.mean(rows, axis=-1, keepdims=True)
+    spread = lax.rsqrt(jnp.mean(centre * centre, axis=-1, keepdims=True) + EPS_NORM)
+    return centre * spread, spread
+
+
+def dense_kernel(
+    homed, cotangent, context, vec, w_out, w_up, w_down,
+    result, grad_one_ref, grad_context, g_out, g_up, g_down, vec_grads,
+    act, slope, hidden_low,
+):
+    width = homed.shape[1]
+    chunks = w_up.shape[4] // width
+    f32 = jnp.float32
+    low = jnp.bfloat16
+
+    def columns(ref, c):
+        return ref[:, :, :, :, c * width : (c + 1) * width].reshape(width, width)
+
+    def keep(n, line):
+        vec_grads[n : n + 1] = jnp.sum(line, axis=0, keepdims=True)
+
+    attn_out = jnp.dot(context[...], columns(w_out, 0), preferred_element_type=f32) + vec[2:3]
+    normed_one, spread_one = normed_rows(homed[...].astype(f32) + attn_out)
+    hidden = normed_one * vec[3:4] + vec[4:5]
+    hidden_low[...] = hidden.astype(low)
+    branch = None
+    for c in range(chunks):
+        pre = jnp.dot(hidden_low[...], columns(w_up, c), preferred_element_type=f32) + vec[8 + c : 9 + c]
+        below = 0.5 * (1.0 + lax.erf(pre * 0.7071067811865476))
+        act[c] = (pre * below).astype(low)
+        slope[c] = below + pre * (jnp.exp(-0.5 * pre * pre) * 0.3989422804014327)
+        part = jnp.dot(act[c], w_down[c].reshape(width, width), preferred_element_type=f32)
+        branch = part if branch is None else branch + part
+    normed_two, spread_two = normed_rows(hidden + branch + vec[5:6])
+    result[...] = (normed_two * vec[6:7] + vec[7:8]).astype(low)
+
+    def back(e, normed, spread, gain):
+        scaled = e * gain
+        return spread * (
+            scaled
+            - jnp.mean(scaled, axis=-1, keepdims=True)
+            - normed * jnp.mean(scaled * normed, axis=-1, keepdims=True)
+        )
+
+    e = cotangent[...].astype(f32)
+    keep(6, e * normed_two)
+    keep(7, e)
+    grad_two = back(e, normed_two, spread_two, vec[6:7])
+    grad_branch = grad_two.astype(low)
+    keep(5, grad_branch.astype(f32))
+    grad_hidden = grad_two
+    for c in range(chunks):
+        g_down[c] = (
+            lax.dot_general(act[c], grad_branch, TN, preferred_element_type=f32)
+            .astype(low)
+            .reshape(g_down.shape[1:])
+        )
+        grad_act = lax.dot_general(
+            grad_branch, w_down[c].reshape(width, width), NT, preferred_element_type=f32
+        )
+        grad_pre = (grad_act * slope[c]).astype(low)
+        keep(8 + c, grad_pre.astype(f32))
+        g_up[:, :, :, :, c * width : (c + 1) * width] = (
+            lax.dot_general(hidden_low[...], grad_pre, TN, preferred_element_type=f32)
+            .astype(low)
+            .reshape(*g_up.shape[:4], width)
+        )
+        grad_hidden = grad_hidden + lax.dot_general(
+            grad_pre, columns(w_up, c), NT, preferred_element_type=f32
+        )
+    keep(3, grad_hidden * normed_one)
+    keep(4, grad_hidden)
+    grad_one = back(grad_hidden, normed_one, spread_one, vec[3:4])
+    grad_one_ref[...] = grad_one
+    grad_attn = grad_one.astype(low)
+    keep(2, grad_attn.astype(f32))
+    g_out[...] = (
+        lax.dot_general(context[...], grad_attn, TN, preferred_element_type=f32)
+        .astype(low)
+        .reshape(g_out.shape)
+    )
+    grad_context[...] = lax.dot_general(
+        grad_attn, columns(w_out, 0), NT, preferred_element_type=f32
+    ).astype(low)
+    vec_grads[0:2] = jnp.zeros((2, width), f32)
+    vec_grads[12:] = jnp.zeros((vec_grads.shape[0] - 12, width), f32)
+
+
+def dense(homed, cotangent, context, vec, w_out, w_up, w_down):
+    tokens, width = homed.shape
+    chunks = w_up.shape[4] // width
+    low = jnp.bfloat16
+    row_shape = jax.ShapeDtypeStruct((tokens, width), low)
+    return pl.pallas_call(
+        dense_kernel,
+        out_shape=[row_shape, jax.ShapeDtypeStruct((tokens, width), jnp.float32), row_shape]
+        + [jax.ShapeDtypeStruct(w.shape, low) for w in (w_out, w_up, w_down)]
+        + [jax.ShapeDtypeStruct((128, width), jnp.float32)],
+        in_specs=vmem(7),
+        out_specs=vmem(7),
+        scratch_shapes=[
+            pltpu.VMEM((chunks, tokens, width), low),
+            pltpu.VMEM((chunks, tokens, width), jnp.float32),
+            pltpu.VMEM((tokens, width), low),
+        ],
+        compiler_params=pltpu.CompilerParams(vmem_limit_bytes=60 << 20),
+        name="dense",
+    )(homed, cotangent, context, vec, w_out, w_up, w_down)
+
+
+LAST = 13
 
 
 def outbound_kernel(
-    result_ref, grad_ref, home_line, slot_column, table_ref, g_qkv, g_out, g_up, g_down,
+    result_ref, grad_one, qkv, grad_context, homed, vec_grads, home_line, slot_column, tables, codes, flipped,
+    w_qkv, g_out, g_up, g_down,
     result_out, grad_out, table_out, o_qkv, o_out, o_up, o_down,
-    packed_a, arrived_a, packed_b, arrived_b, table_got,
+    packed, arrived_a, arrived_b, table_got, grad_qkv, g_qkv,
     t_qkv, t_out, t_up, t_down, c_qkv, c_out, c_up, c_down, n_qkv, n_out, n_up, n_down,
     f_qkv, f_out, f_up, f_down, z_qkv, z_out, z_up, z_down, e_qkv, e_out, e_up, e_down,
-    send_a, recv_a, send_b, recv_b, local_sems, table_sems, piece_sems, last_sems,
+    send_a, recv_a, send_b, recv_b, local_sems, table_sems, piece_sems, fetch_sems, last_sems,
 ):
     where = place()
     me, core, z, y, x = where
@@ -604,37 +919,72 @@
     from_z = (z_qkv, z_out, z_up, z_down)
     ends = (e_qkv, e_out, e_up, e_down)
     outs = (o_qkv, o_out, o_up, o_down)
+    low = jnp.bfloat16
     tasks = []
     for i in (3, 2, 1, 0):
-        for piece in pieces_of(sums[i].shape[3], sums[i].shape[4]):
+        refs = (local[i], sums[i], from_core[i], from_near[i], from_far[i], from_z[i])
+        for pair in pieces_of(sums[i].shape[3], sums[i].shape[4]):
             n = len(tasks)
-            tasks.append(
-                Scatter(where, local[i], sums[i], from_core[i], from_near[i], from_far[i], from_z[i], piece, piece_sems.at[n])
-            )
-    moved = Exchange(where, packed_a, arrived_a, send_a, recv_a, local_sems.at[0])
-    moved_grad = Exchange(where, packed_b, arrived_b, send_b, recv_b, local_sems.at[1])
-    table_out[...] = table_ref[...]
-    steps = [(me, 1 - core), (me ^ 1, core), (me ^ 2, core), (me ^ 4, core), (me ^ 8, core)]
+            pair = [
+                Scatter(where, *refs, fetch_sems.at[2 * n + j], piece, piece_sems.at[2 * n + j])
+                for j, piece in enumerate(pair)
+            ]
+            tasks.append((pair, n if i else LAST + n - 5, Scatter.OFFSETS))
+    step, steps = stepper(tasks)
+    moved = Exchange(where, packed, arrived_a, send_a, recv_a, local_sems.at[0])
+    moved_grad = Exchange(where, packed, arrived_b, send_b, recv_b, local_sems.at[1])
+    devices = [(me, 1 - core), (me ^ 1, core), (me ^ 2, core), (me ^ 4, core), (me ^ 8, core)]
     shares = [
         remote(table_got.at[0, n], table_got.at[1, n], table_sems.at[0, n], table_sems.at[1, n], device)
-        for n, device in enumerate(steps)
+        for n, device in enumerate(devices)
     ]
 
-    def extra(k):
-        if k == 0:
-            moved.pack(result_ref, home_line)
-        if k == 3:
-            moved_grad.pack(grad_ref, home_line)
-        if 4 <= k <= 9:
-            n = k - 4
-            if n > 0:
-                shares[n - 1].wait_recv()
-                table_out[...] += table_got[1, n - 1]
-            if n < 5:
-                table_got[0, n] = table_out[...]
-                shares[n].start()
-
-    staggered(tasks, 7, extra)
+    step(0)
+    moved.pack(result_ref, home_line)
+
+    def one(pair, carry):
+        attend_pair_back(pair, qkv, grad_context, tables, codes, flipped, grad_qkv, table_out)
+        for j in range(PAIRS):
+
+            @pl.when(pair == j)
+            def _(j=j):
+                step(1 + 2 * j)
+                step(2 + 2 * j)
+
+        return carry
+
+    lax.fori_loop(0, PAIRS, one, 0)
+    width = homed.shape[1]
+    sums_of = []
+    in_home = grad_one[...]
+    for n in range(3):
+        part = grad_qkv[:, n * width : (n + 1) * width]
+        g_qkv[:, :, :, :, n * width : (n + 1) * width] = (
+            lax.dot_general(homed[...], part, TN, preferred_element_type=jnp.float32)
+            .astype(low)
+            .reshape(*g_qkv.shape[:4], width)
+        )
+        sums_of.append(jnp.sum(part.astype(jnp.float32), axis=0, keepdims=True))
+        weights = w_qkv[:, :, :, :, n * width : (n + 1) * width].reshape(width, width)
+        in_home = in_home + lax.dot_general(part, weights, NT, preferred_element_type=jnp.float32)
+    row = lax.broadcasted_iota(jnp.int32, (128, width), 0)
+    lines = jnp.where(row == 0, sums_of[0], jnp.where(row == 1, sums_of[2], vec_grads[...]))
+    beside = lines.T.astype(low).reshape(*g_qkv.shape[:4], 128)
+    g_qkv[:, :, :, :, 3 * width : 3 * width + 128] = beside
+    g_qkv[:, :, :, :, 3 * width + 128 :] = jnp.zeros_like(beside)
+    step(LAST)
+    moved.wait()
+    moved_grad.pack_value(in_home.astype(low), home_line)
+    moved.unpack(slot_column, result_out, low)
+    for k in range(LAST + 1, steps):
+        step(k)
+        n = k - LAST - 1
+        if 0 < n <= 5:
+            shares[n - 1].wait_recv()
+            table_out[...] += table_got[1, n - 1]
+        if n < 5:
+            table_got[0, n] = table_out[...]
+            shares[n].start()
     finals = []
     for i in (3, 2, 1, 0):
         block = sums[i][z, y, x].astype(jnp.float32)
@@ -645,27 +995,27 @@
         copy = remote(ends[i].at[1 - core], outs[i].at[core], last_sems.at[0, i], last_sems.at[1, i], (me, 1 - core))
         copy.start()
         finals.append(copy)
-    moved.wait()
-    moved.unpack(slot_column, result_out, jnp.bfloat16)
     moved_grad.wait()
     moved_grad.unpack(slot_column, grad_out, jnp.float32)
     for copy in finals:
         copy.wait()
     for share in shares:
         share.wait_send()
-    for task in tasks:
-        task.sent()
-
-
-def outbound(result, grads, home_line, slot_column, table, locals_):
+    for pair, _, _ in tasks:
+        for task in pair:
+            task.sent()
+
+
+def outbound(result, grad_one, qkv, grad_context, homed, vec_grads, home_line, slot_column, tables, codes, flipped, w_qkv, locals_):
     tokens, width = result.shape
     slots = 2 * (2 * tokens // PEERS)
-    buffer = pltpu.VMEM((PEERS, slots, width // 2), jnp.bfloat16)
-    halves = [(g.shape[3], g.shape[4] // 2) for g in locals_]
     low = jnp.bfloat16
+    buffer = pltpu.VMEM((PEERS, slots, width // 2), low)
+    halves = [(g.shape[3], g.shape[4] // 2) for g in (w_qkv, *locals_)]
     scratch = (
-        [buffer] * 4
-        + [pltpu.VMEM((2, 5, *table.shape), jnp.float32)]
+        [buffer] * 3
+        + [pltpu.VMEM((2, 5, *tables.shape), jnp.float32)]
+        + [pltpu.VMEM(qkv.shape, low), pltpu.VMEM(w_qkv.shape, low)]
         + [pltpu.VMEM((4, 2, 2, r, h), low) for r, h in halves]
         + [pltpu.VMEM((4, 2, 2, r, h), low) for r, h in halves]
         + [pltpu.VMEM((4, 2, r, h), low) for r, h in halves]
@@ -677,20 +1027,20 @@
     return pl.pallas_call(
         outbound_kernel,
         out_shape=[
-            jax.ShapeDtypeStruct(result.shape, jnp.bfloat16),
+            jax.ShapeDtypeStruct(result.shape, low),
             jax.ShapeDtypeStruct(result.shape, jnp.float32),
-            jax.ShapeDtypeStruct(table.shape, jnp.float32),
+            jax.ShapeDtypeStruct(tables.shape, jnp.float32),
         ]
         + [jax.ShapeDtypeStruct((2, r // 2, h), jnp.float32) for r, h in halves],
-        in_specs=vmem(9),
+        in_specs=vmem(12) + [pl.BlockSpec(memory_space=pl.ANY)] * 3,
         out_specs=vmem(7),
         scratch_shapes=scratch
-        + [dma((PEERS,)), dma((PEERS,)), dma((PEERS,)), dma((PEERS,)), dma((2,)), dma((2, 5)), dma((8, 2, 5)), dma((2, 4))],
+        + [dma((PEERS,)), dma((PEERS,)), dma((PEERS,)), dma((PEERS,)), dma((2,)), dma((2, 5)), dma((14, 2, 5)), dma((14,)), dma((2, 4))],
         compiler_params=pltpu.CompilerParams(
-            collective_id=2, has_side_effects=True, vmem_limit_bytes=60 << 20
+            collective_id=2, has_side_effects=True, vmem_limit_bytes=62 << 20
         ),
         name="outbound",
-    )(result, grads, home_line, slot_column, table, *locals_)
+    )(result, grad_one, qkv, grad_context, homed, vec_grads, home_line, slot_column, tables, codes, flipped, w_qkv, *locals_)
 
 
 def shard_halves(shard):
@@ -699,17 +1049,128 @@
     return (rows, jnp.pad(halves, ((0, 0), (0, -rows % 16), (0, 0))))
 
 
-def chip_blocks(grad):
-    rows, columns = grad.shape
-    return grad.astype(jnp.bfloat16).reshape(4, 2, 2, rows // PEERS, columns)
-
-
 def joined(halves):
     return jnp.concatenate([halves[0], halves[1]], axis=1)
 
 
 def per_device(
-    kernels,
+    layer_in,
+    out_grad,
+    w_qkv,
+    w_out,
+    w_up,
+    w_down,
+    vectors,
+    relative,
+    first_qkv,
+    second_qkv,
+    first_out,
+    second_out,
+    first_up,
+    second_up,
+    first_down,
+    second_down,
+    first_vectors,
+    second_vectors,
+    first_relative,
+    second_relative,
+    token_slot,
+    home_index,
+    box_x,
+    box_y,
+):
+    tokens = layer_in[0]
+    rows_dev, model_dim = tokens.shape
+    slot_cap = 2 * rows_dev // lax.axis_size("regions")
+    kinds = vectors.shape[0]
+    beside = jnp.pad(vectors.T, ((0, 0), (0, VEC_COLS - kinds)))
+    wide_qkv = jnp.concatenate([w_qkv, beside], axis=1)
+    slot_at = token_slot[0] + slot_cap * (token_slot[0] // slot_cap)
+    home_at = home_index[0] + slot_cap * (home_index[0] // slot_cap)
+    bucket = jnp.arange(PAGE, dtype=jnp.int32) * 64 // PAGE
+    codes = code_columns(bucket, box_x[0], box_y[0])
+    flipped = code_columns(63 - bucket, 31 - box_x[0], 31 - box_y[0])
+    tables = table_lines(relative)
+    homed, cotangent, qkv, context, vec, whole_qkv, whole_out, whole_up, whole_down = inbound(
+        tokens,
+        out_grad[0],
+        slot_at[None],
+        home_at[:, None],
+        tables,
+        codes,
+        [shard_halves(shard) for shard in (wide_qkv, w_out, w_up, w_down)],
+    )
+    result, grad_one, grad_context, local_out, local_up, local_down, vec_grads = dense(
+        homed, cotangent, context, vec, whole_out, whole_up, whole_down
+    )
+    layer_out, in_grad, table_sum, *ends = outbound(
+        result,
+        grad_one,
+        qkv,
+        grad_context,
+        homed,
+        vec_grads,
+        home_at[None],
+        slot_at[:, None],
+        tables,
+        codes,
+        flipped,
+        whole_qkv,
+        [local_out, local_up, local_down],
+    )
+    grad_relative = lines_back(table_sum)
+    grad_qkv, grad_out, grad_up, grad_down = [joined(end) for end in ends]
+    grad_vectors = grad_qkv[:, 3 * model_dim : 3 * model_dim + kinds].T
+    grad_qkv = grad_qkv[:, : 3 * model_dim]
+    firsts_qkv, seconds_qkv, update_qkv = adam_step(
+        w_qkv.astype(jnp.float32), grad_qkv, first_qkv, second_qkv, DECAY_RATE
+    )
+    firsts_out, seconds_out, update_out = adam_step(
+        w_out.astype(jnp.float32), grad_out, first_out, second_out, DECAY_RATE
+    )
+    firsts_up, seconds_up, update_up = adam_step(
+        w_up.astype(jnp.float32), grad_up, first_up, second_up, DECAY_RATE
+    )
+    firsts_down, seconds_down, update_down = adam_step(
+        w_down.astype(jnp.float32), grad_down, first_down, second_down, DECAY_RATE
+    )
+    firsts_vectors, seconds_vectors, update_vectors = adam_step(
+        vectors.astype(jnp.float32), grad_vectors, first_vectors, second_vectors, 0.0
+    )
+    firsts_relative, seconds_relative, update_relative = adam_step(
+        relative, grad_relative, first_relative, second_relative, 0.0
+    )
+    return (
+        layer_out[None],
+        in_grad[None],
+        grad_qkv,
+        firsts_qkv,
+        seconds_qkv,
+        update_qkv,
+        grad_out,
+        firsts_out,
+        seconds_out,
+        update_out,
+        grad_up,
+        firsts_up,
+        seconds_up,
+        update_up,
+        grad_down,
+        firsts_down,
+        seconds_down,
+        update_down,
+        grad_vectors,
+        firsts_vectors,
+        seconds_vectors,
+        update_vectors,
+        grad_relative,
+        firsts_relative,
+        seconds_relative,
+        update_relative,
+    )
+
+
+def spread_device(
     layer_in,
     out_grad,
     w_qkv,
@@ -743,38 +1204,19 @@
     page_num = rows_dev // PAGE
     slot_of = token_slot[0]
     home_rows = home_index[0]
-    if kernels:
-        beside = jnp.pad(vectors.T, ((0, 0), (0, VEC_COLS - vectors.shape[0])))
-        wide_qkv = jnp.concatenate([w_qkv, beside], axis=1)
-        slot_at = slot_of + slot_cap * (slot_of // slot_cap)
-        home_at = home_rows + slot_cap * (home_rows // slot_cap)
-        homed, cotangent, *fulls = inbound(
-            tokens,
-            out_grad[0],
-            slot_at[None],
-            home_at[:, None],
-            [shard_halves(shard) for shard in (wide_qkv, w_out, w_up, w_down)],
-        )
-        cotangent = cotangent.astype(jnp.float32)
-        full_qkv, full_out, full_up, full_down = [
-            full.reshape(-1, full.shape[4]) for full in fulls
-        ]
-        full_vec = full_qkv[:, 3 * model_dim : 3 * model_dim + vectors.shape[0]].T
-        full_qkv = full_qkv[:, : 3 * model_dim]
-    else:
-        full_qkv, full_out, full_up, full_down, full_vec = (
-            lax.all_gather(w_qkv, ("regions", "shard"), axis=0, tiled=True),
-            lax.all_gather(w_out, ("regions", "shard"), axis=0, tiled=True),
-            lax.all_gather(w_up, ("regions", "shard"), axis=0, tiled=True),
-            lax.all_gather(w_down, ("regions", "shard"), axis=0, tiled=True),
-            lax.all_gather(vectors, ("regions", "shard"), axis=1, tiled=True),
-        )
-        homed = exchange(tokens, slot_of, home_rows, groups, slot_cap).astype(jnp.bfloat16)
-        cotangent = exchange(out_grad[0], slot_of, home_rows, groups, slot_cap)
+    full_qkv, full_out, full_up, full_down, full_vec = (
+        lax.all_gather(w_qkv, ("regions", "shard"), axis=0, tiled=True),
+        lax.all_gather(w_out, ("regions", "shard"), axis=0, tiled=True),
+        lax.all_gather(w_up, ("regions", "shard"), axis=0, tiled=True),
+        lax.all_gather(w_down, ("regions", "shard"), axis=0, tiled=True),
+        lax.all_gather(vectors, ("regions", "shard"), axis=1, tiled=True),
+    )
     vec_rows = full_vec.astype(jnp.float32)
     qkv_bias = jnp.concatenate([vec_rows[0], jnp.zeros_like(vec_rows[0]), vec_rows[1]])
     code_rows = position_codes(box_x[0].reshape(page_num, PAGE), box_y[0].reshape(page_num, PAGE))
     bias_mats = bias_table(relative)
+    homed = exchange(tokens, slot_of, home_rows, groups, slot_cap).astype(jnp.bfloat16)
+    cotangent = exchange(out_grad[0], slot_of, home_rows, groups, slot_cap)
     projected = (jnp.dot(homed, full_qkv, preferred_element_type=jnp.float32) + qkv_bias).astype(
         jnp.bfloat16
     )
@@ -825,6 +1267,8 @@
     in_home = grad_one + jnp.einsum(
         "tf,df->td", grad_dense, full_qkv, preferred_element_type=jnp.float32
     )
+    layer_out = exchange(result.astype(jnp.bfloat16), home_rows, slot_of, groups, slot_cap)
+    in_grad = exchange(in_home.astype(jnp.bfloat16), home_rows, slot_of, groups, slot_cap)
     grad_vec = jnp.concatenate(
         [
             jnp.stack(
@@ -843,42 +1287,16 @@
         ],
         axis=0,
     )
+    grad_qkv, grad_out, grad_up, grad_down, grad_vectors = (
+        lax.psum_scatter(grad_qkv, ("regions", "shard"), scatter_dimension=0, tiled=True),
+        lax.psum_scatter(grad_out, ("regions", "shard"), scatter_dimension=0, tiled=True),
+        lax.psum_scatter(grad_up, ("regions", "shard"), scatter_dimension=0, tiled=True),
+        lax.psum_scatter(grad_down, ("regions", "shard"), scatter_dimension=0, tiled=True),
+        lax.psum_scatter(grad_vec, ("regions", "shard"), scatter_dimension=1, tiled=True),
+    )
     mats_total = jnp.sum(mats_pages, axis=0)
     table_back = jax.vjp(bias_table, relative)[1]
-    table_local = table_back(mats_total)[0]
-    if kernels:
-        beside = jnp.pad(grad_vec.T, ((0, 0), (0, VEC_COLS - grad_vec.shape[0])))
-        heads, entries = relative.shape
-        layer_out, in_grad, table_sum, *ends = outbound(
-            result.astype(jnp.bfloat16),
-            in_home.astype(jnp.bfloat16),
-            home_at[None],
-            slot_at[:, None],
-            jnp.pad(table_local, ((0, -heads % 8), (0, -entries % 128))),
-            [
-                chip_blocks(grad)
-                for grad in (
-                    jnp.concatenate([grad_qkv, beside], axis=1),
-                    grad_out,
-                    grad_up,
-                    grad_down,
-                )
-            ],
-        )
-        grad_relative = table_sum[:heads, :entries]
-        grad_qkv, grad_out, grad_up, grad_down = [joined(end) for end in ends]
-        grad_vectors = grad_qkv[:, 3 * model_dim : 3 * model_dim + vectors.shape[0]].T
-        grad_qkv = grad_qkv[:, : 3 * model_dim]
-    else:
-        layer_out = exchange(result.astype(jnp.bfloat16), home_rows, slot_of, groups, slot_cap)
-        in_grad = exchange(in_home.astype(jnp.bfloat16), home_rows, slot_of, groups, slot_cap)
-        over = ("regions", "shard")
-        grad_qkv, grad_out, grad_up, grad_down = [
-            lax.psum_scatter(grad, over, scatter_dimension=0, tiled=True)
-            for grad in (grad_qkv, grad_out, grad_up, grad_down)
-        ]
-        grad_vectors = lax.psum_scatter(grad_vec, over, scatter_dimension=1, tiled=True)
-        grad_relative = lax.psum(table_local, over)
+    grad_relative = lax.psum(table_back(mats_total)[0], ("regions", "shard"))
     firsts_qkv, seconds_qkv, update_qkv = adam_step(
         w_qkv.astype(jnp.float32), grad_qkv, first_qkv, second_qkv, DECAY_RATE
     )
@@ -930,7 +1348,7 @@
 def solution(mesh):
     kernels = mesh.shape["regions"] == PEERS and mesh.shape["shard"] == 2
     return jax.shard_map(
-        functools.partial(per_device, kernels),
+        per_device if kernels else spread_device,
         mesh=mesh,
         in_specs=(
             P("shard", "regions", None),

time: 648 us -> 388 us (0.60)
  matrix products: 144 us -> 0 us
  Pallas kernels: 402 us -> 351 us
  local copies, waits for them, and re-layouts: 49.4 us -> 14.8 us
  other arithmetic: 40.2 us -> 13.6 us
    dot_general x22 -> x0, matrix products: 144 us -> none  [the longest x1 22.8 us: per_device(): jnp.dot(hidden_low, full_up, preferred_element_type=jnp.float32)]
    pallas_call x1, Pallas kernels: 198 us -> 158 us  [outbound(): pl.pallas_call(outbound_kernel, out_shape=[jax.ShapeDtypeStruct(result.sh...]
    reduce_sum x10 -> x0, other arithmetic: 15.9 us -> none  [the longest x1 8.49 us: page_forward(): totals = jnp.sum(raised, axis=2, keepdims=True)]
    convert_element_type x2 -> x1, other arithmetic: 12.2 us -> 1.75 us  [code_columns(): return hit.astype(jnp.bfloat16)]
    pallas_call x1 -> x2, Pallas kernels: 204 us -> 194 us  [the longest x1 162 us: inbound(): pl.pallas_call(inbound_kernel, out_shape=[jax.ShapeDtypeStruct((tokens, w...]
    another operation x8 -> x3, local copies, waits for them, and re-layouts: 8.42 us -> 0.02 us  [table_lines(): return jnp.pad(jnp.stack(lines, axis=1), ((0, 0), (0, 5), (0, 0)))]
where the time goes in v3:
time: 388 us; the launch traced here: 381 us
  Pallas kernels  351 us (90%)
  local copies, waits for them, and re-layouts  14.8 us (4%)
  other arithmetic  13.6 us (4%)
    pallas_call x1, Pallas kernels, inbound(): pl.pallas_call(inbound_kernel, out_shape=[jax.ShapeDtypeStruct((tokens, w...  162 us
    pallas_call x1, Pallas kernels, outbound(): pl.pallas_call(outbound_kernel, out_shape=[jax.ShapeDtypeStruct(result.sh...  158 us
    pallas_call x1, Pallas kernels, dense(): pl.pallas_call(dense_kernel, out_shape=[row_shape, jax.ShapeDtypeStruct((...  31.8 us

profile of v3, /device:TPU:0, one launch (start us, length us, event | category | flops | bytes accessed | tf_op | source)
XLA Modules:
  0.0 381.0 jit_solution(14190901914329238442)
XLA Ops:
  0.7 0.8 subtract_reduce_fusion.1
  1.5 0.7 subtract_reduce_fusion
  2.2 1.8 fusion.4
  4.0 0.7 slice_select_fusion
  4.7 0.1 slice.100
  4.7 0.1 pad_maximum_fusion.5
  4.8 0.8 fusion.25
  5.7 0.1 concatenate.35
  5.8 0.1 concatenate.36
  5.8 0.6 select_maximum_fusion.tables
  6.5 0.7 fusion.17
  7.2 0.2 copy.79
  7.4 0.8 copy.78
  8.2 0.8 add.201.home_column
  9.0 0.8 copy.98
  9.7 0.9 fusion.10
  10.7 0.7 pad.35.s_qkv
  11.4 0.7 pad.37.s_up
  12.0 0.7 copy.110
  12.7 0.6 pad.36.s_out
  13.4 0.6 multiply_add_fusion.7.slot_line
  14.0 162.0 %inbound.1 = (bf16[576,768]{1,0:T(8,128)(2,1)}, bf16[576,768]{1,0:T(8,128)(2,1)}, bf16[576,2304]{1,0:T(8,128)(2,1)}, bf16[576,768]{1,0:T(8,128)(2,1)}, f32[16,76...) custom-call(bf16[576,768]{1,0:T(8,128)(2,1)} %bitcast.74, ...), custom_call_target="tpu_custom_call" | custom-call | tf_op jit(solution)/shard_map/inbound/pallas_call | solution.py:767
  176.0 0.0 copy-start.19
  176.0 31.8 %dense.1 = (bf16[576,768]{1,0:T(8,128)(2,1)}, f32[576,768]{1,0:T(8,128)}, bf16[576,768]{1,0:T(8,128)(2,1)}, bf16[4,2,2,48,768]{4,3,2,1,0:T(8,128)(2,1)}, bf16[4,...) custom-call(bf16[576,768]{1,0:T(8,128)(2,1)} %get-tuple-element.49.homed, ...), custom_call_target="tpu_custom_call" | custom-call | tf_op jit(solution)/shard_map/dense/pallas_call | solution.py:882
  207.8 0.2 copy.86
  207.9 0.2 copy.85
  208.1 0.8 add.207.slot_column
  208.8 0.6 multiply_add_fusion.6.home_line
  209.5 157.7 %outbound.1 = (bf16[576,768]{1,0:T(8,128)(2,1)}, f32[576,768]{1,0:T(8,128)}, f32[12,8,128]{2,1,0:T(8,128)}, f32[2,24,1280]{2,1,0:T(8,128)}, f32[2,24,384]{2,1,0:...) custom-call(bf16[576,768]{1,0:T(8,128)(2,1)} %get-tuple-element.56.result_ref, ...), custom_call_target="tpu_custom_call" | custom-call | tf_op jit(solution)/shard_map/outbound/pallas_call | solution.py:1027
  367.2 0.9 slice.96
  368.1 0.1 slice.103
  368.2 0.9 slice.95
  369.1 0.8 slice.94
  369.9 0.7 add_multiply_fusion.4
  370.6 1.0 slice_bitcast_fusion.1
  371.7 1.1 add_multiply_fusion
  372.9 1.1 add_multiply_fusion.1
  374.0 0.7 add_multiply_fusion.3
  374.8 1.0 add_multiply_fusion.2
  375.7 0.1 copy.87
  375.8 0.1 copy.89
  375.9 0.1 copy.90
  376.0 0.7 copy.92
  376.7 0.7 copy.93
  377.4 0.7 copy.94
  378.1 0.7 copy.91
  378.7 0.9 copy.119
  379.6 1.2 copy.120
  (67 shorter events, 0.3 us)
Async XLA Ops:
  0.7 10.7 %copy-start.3 = (bf16[24,3072]{1,0:T(8,128)(2,1)S(1)}, bf16[24,3072]{1,0:T(8,128)(2,1)}, u32[]{:S(2)}) copy-start(bf16[24,3072]{1,0:T(8,128)(2,1)} %param.28) | copy-start | bytes 442372
  0.7 11.4 %copy-start.2 = (bf16[96,768]{1,0:T(8,128)(2,1)S(1)}, bf16[96,768]{1,0:T(8,128)(2,1)}, u32[]{:S(2)}) copy-start(bf16[96,768]{1,0:T(8,128)(2,1)} %param.29) | copy-start | bytes 442372
  0.7 12.0 %copy-start.13 = (bf16[24,768]{1,0:T(8,128)(2,1)S(1)}, bf16[24,768]{1,0:T(8,128)(2,1)}, u32[]{:S(2)}) copy-start(bf16[24,768]{1,0:T(8,128)(2,1)} %param.27) | copy-start | bytes 110596
  0.7 12.7 %copy-start.18 = (s32[1,576]{1,0:T(1,128)S(1)}, s32[1,576]{1,0:T(1,128)}, u32[]{:S(2)}) copy-start(s32[1,576]{1,0:T(1,128)} %param.44) | copy-start | bytes 6916
  176.0 32.9 %copy-start.19 = (s32[1,576]{1,0:T(1,128)S(1)}, s32[1,576]{1,0:T(1,128)}, u32[]{:S(2)}) copy-start(s32[1,576]{1,0:T(1,128)} %param.45) | copy-start | bytes 6916
  209.4 160.4 %copy-start.14 = (f32[12,253]{1,0:T(8,128)S(1)}, f32[12,253]{1,0:T(8,128)}, u32[]{:S(2)}) copy-start(f32[12,253]{1,0:T(8,128)} %param.31) | copy-start | bytes 36436
  209.4 160.4 %copy-start.20 = (f32[12,253]{1,0:T(8,128)S(1)}, f32[12,253]{1,0:T(8,128)}, u32[]{:S(2)}) copy-start(f32[12,253]{1,0:T(8,128)} %param.43) | copy-start | bytes 36436
  209.4 160.4 %copy-start.21 = (f32[12,253]{1,0:T(8,128)S(1)}, f32[12,253]{1,0:T(8,128)}, u32[]{:S(2)}) copy-start(f32[12,253]{1,0:T(8,128)} %param.42) | copy-start | bytes 36436
  209.5 162.2 %copy-start.5 = (f32[96,768]{1,0:T(8,128)S(1)}, f32[96,768]{1,0:T(8,128)}, u32[]{:S(2)}) copy-start(f32[96,768]{1,0:T(8,128)} %param.39) | copy-start | bytes 884740
  209.5 162.2 %copy-start.6 = (f32[96,768]{1,0:T(8,128)S(1)}, f32[96,768]{1,0:T(8,128)}, u32[]{:S(2)}) copy-start(f32[96,768]{1,0:T(8,128)} %param.38) | copy-start | bytes 884740
  367.2 5.6 %copy-start.9 = (f32[2,24,1536]{2,1,0:T(8,128)S(1)}, f32[2,24,1536]{2,1,0:T(8,128)}, u32[]{:S(2)}) copy-start(f32[2,24,1536]{2,1,0:T(8,128)} %get-tuple-element.69) | copy-start | bytes 884740
  367.2 5.6 %copy-start.7 = (f32[24,3072]{1,0:T(8,128)S(1)}, f32[24,3072]{1,0:T(8,128)}, u32[]{:S(2)}) copy-start(f32[24,3072]{1,0:T(8,128)} %param.37) | copy-start | bytes 884740
  367.2 5.6 %copy-start.8 = (f32[24,3072]{1,0:T(8,128)S(1)}, f32[24,3072]{1,0:T(8,128)}, u32[]{:S(2)}) copy-start(f32[24,3072]{1,0:T(8,128)} %param.36) | copy-start | bytes 884740
  371.6 2.3 copy-start.17
  371.6 2.4 copy-start.15
  371.6 2.3 copy-start.16
  371.7 3.1 copy-start.10
  371.7 3.1 copy-start.4
  371.7 3.1 copy-start.11
  371.7 3.1 copy-start.12
  372.8 2.9 copy-start.23
  372.8 3.0 copy-start.24
  372.8 3.1 copy-start.22
  372.9 5.9 %copy-start.1 = (bf16[576,768]{1,0:T(8,128)(2,1)S(1)}, bf16[576,768]{1,0:T(8,128)(2,1)}, u32[]{:S(2)}) copy-start(bf16[576,768]{1,0:T(8,128)(2,1)} %get-tuple-element.65) | copy-start | bytes 2654212
  374.0 5.7 %copy-start = (f32[576,768]{1,0:T(8,128)S(1)}, f32[576,768]{1,0:T(8,128)}, u32[]{:S(2)}) copy-start(f32[576,768]{1,0:T(8,128)} %get-tuple-element.66) | copy-start | bytes 5308420
